TPU v7x, 256 devices: a whole 4x4x8 slice. The times are simulated.
256 devices in a mesh: wave: 16 (over x, y), ny: 16 (over z, core).
Axes of the slice: x: 4, y: 4, z: 8, core: 2. Of those that a mesh axis runs over, the one named last changes fastest.
Arguments:
- spectra: bfloat16 [640, 48, 1281], P('wave', 'ny'), may hold values from -0.0024414062 to 0.0024414062
- legendre: bfloat16 [640, 256, 1281], P('wave', 'ny'), may hold values from -6 to 6
- lon_anchor: int32 [1], replicated, may hold values from 0 to 5119
- row_index: int32 [2048], P('ny'), may hold values from 0 to 254, as said below
- row_weight: float32 [2048], P('ny'), may hold values from 0 to 1
- col_index: int32 [2048], P('wave'), may hold values from 0 to 510, as said below
- col_weight: float32 [2048], P('wave'), may hold values from 0 to 1
- zone_width: int32 [4], replicated, may hold values from 8 to 16, as said below
- nest_state: bfloat16 [24, 2048, 2048], P(None, 'ny', 'wave'), may hold values from -6 to 6
Outputs:
- parent_band: float32 [24, 256, 512], P(None, 'ny', 'wave')
- nest_next: bfloat16 [24, 2048, 2048], P(None, 'ny', 'wave')
Inputs may be any that keep to these rules, and one draw needn't show every extreme that they name: For a nest row in ny block y (rows y * 128 onward), row_index lies from y * 16 - 1 to (y + 1) * 16 - 1; both ends are reached in every block that is neither the first nor the last. For a nest column in wave block w, col_index lies from w * 32 - 1 to (w + 1) * 32 - 1; both ends are reached in every block that is neither the first nor the last. `zone_width`: at least one side has width exactly 16.
All inputs are finite; a program needn't handle non-finite values.
Results may differ from a plain program's by a relative error of at most 0.001.
Values may be sent and summed in bfloat16 or wider, within the bound.
A program may use at most 128 MiB of HBM per device.

v0:
```python
import functools
import math

import jax
import jax.numpy as jnp
import numpy as np
from jax import lax
from jax.experimental import pallas as pl
from jax.experimental.pallas import tpu as pltpu
from jax.sharding import PartitionSpec as P

MESH = pl.DeviceIdType.MESH
NW = 16
NY = 16
PD = 40
TRUNC = 1280
NLON = 5120
LON = 32
KF = 24
NLB = 512
NSWEEP = 4
DIFFUSION = 0.2
F32 = jnp.float32
BF16 = jnp.bfloat16
CHUNKS = ((0, 8, 0, 32, 8), (8, 16, 32, 48, 0), (24, 16, 80, 48, 0))
PIECES = ((0, 0, 1280), (1, 0, 1280), (2, 0, 1280))
KOFF = (0, 256, 768)
NKEY = 1280
SLOTS = 56
EXT = 144
WIN = 128
MB = 256


def chunk_consts():
    out = []
    for _, n, _, rows, lead in CHUNKS:
        row = np.arange(2 * n * 16)
        col = np.arange(8 * rows)
        inner = col % rows - lead
        ok = (inner >= 0)
        cpair = np.where(ok, inner % n, -1)
        chan = (col // rows) * 3 + np.maximum(inner, 0) // n
        mask = ((row // 16) % n)[:, None] == cpair[None, :]
        fold = np.zeros((2, 2, 8 * rows, 128), np.float32)
        for nb in range(2):
            for i in range(8 * rows):
                if ok[i]:
                    fold[nb, 0, i, nb * 24 + chan[i]] = 1.0
                    fold[nb, 1, i, 48 + nb * 24 + chan[i]] = 1.0
        out.append((mask.astype(np.float32), fold))
    return out


def split2(x):
    hi = x.astype(BF16)
    lo = (x - hi.astype(F32)).astype(BF16)
    return hi, lo


def dot_nt(a, b):
    return lax.dot_general(a, b, (((1,), (1,)), ((), ())), preferred_element_type=F32)


def dot_nn(a, b):
    return lax.dot_general(a, b, (((1,), (0,)), ((), ())), preferred_element_type=F32)


def ramps(pos, first, last, total):
    return jnp.maximum(
        jnp.maximum(0.0, 1.0 - pos / first), jnp.maximum(0.0, 1.0 - (total - 1 - pos) / last)
    )


def shares(row, col, zone_ref):
    z = [zone_ref[i].astype(F32) for i in range(4)]
    share = jnp.maximum(ramps(row, z[0], z[1], 2048.0), ramps(col, z[2], z[3], 2048.0))
    inside = (row >= 0.0) & (row < 2048.0) & (col >= 0.0) & (col < 2048.0)
    inside = jnp.where(inside, 1.0, 0.0)
    return (1.0 - share) * inside, share * inside


def k1(
    anchor_ref, zone_ref, spec_ref, leg_ref, mask_a, mask_b, fold_a, fold_b, nest_ref,
    ridx_ref, rwt_ref, cidx_ref, cwt_ref,
    win_out, field_out, info_out,
    gath, sp32, leg2, legx, fs, fsend, frecv, tcos, tsin, acc_c, acc_s, psend, prow, pbuf,
    ext, damp, cpk_s, cpk_r, rpk, rpk_s, rpk_r, info_s, info_r, nest_s, nest_r,
    up_s, up_r, dn_s, dn_r, sib_s, sib_r, fa_s, fa_r, w_s, w_r,
):
    w = lax.axis_index("wave")
    y = lax.axis_index("ny")
    wedge = jnp.logical_or(w == 0, w == NW - 1)

    def near(d):
        return lax.rem(y + (NY + d), NY)

    def dev(ww, yy):
        return (ww, yy)

    up_y = lax.rem(y + 2, NY)
    dn_y = lax.rem(y + NY - 2, NY)
    sib_y = y + 1 - 2 * lax.rem(y, 2)

    def zero(i, c):
        pbuf[i] = jnp.zeros((KF, WIN), F32)
        return c
    lax.fori_loop(0, SLOTS, zero, 0)
    cpk_r[...] = jnp.zeros((2, 128, 128), BF16)
    rpk_r[...] = jnp.zeros((2, 96, 256), BF16)
    info_r[...] = jnp.zeros((4, 8, 128), F32)

    barrier = pltpu.get_barrier_semaphore()

    def greet(ww, yy):
        pl.semaphore_signal(barrier, inc=1, device_id=dev(ww, yy), device_id_type=MESH)

    for yy in (up_y, dn_y, sib_y):
        greet(w, yy)

    def greet_wave(o, c):
        greet(lax.rem(w + o, NW), y)
        return c
    lax.fori_loop(1, NW, greet_wave, 0)

    @pl.when(y > 0)
    def _():
        greet(w, near(-1))

    @pl.when(y < NY - 1)
    def _():
        greet(w, near(1))

    @pl.when(jnp.logical_and(wedge, y > 0))
    def _():
        lax.fori_loop(0, NW, lambda o, c: (greet(o, near(-1)), c)[1], 0)

    @pl.when(jnp.logical_and(wedge, y < NY - 1))
    def _():
        lax.fori_loop(0, NW, lambda o, c: (greet(o, near(1)), c)[1], 0)

    @pl.when(jnp.logical_and(wedge, y > 1))
    def _():
        greet(NW - 1, near(-2))

    @pl.when(jnp.logical_and(wedge, y < NY - 2))
    def _():
        greet(0, near(2))

    @pl.when(jnp.logical_and(jnp.logical_not(wedge), y == 0))
    def _():
        greet(0, 1)

    @pl.when(jnp.logical_and(jnp.logical_not(wedge), y == NY - 1))
    def _():
        greet(NW - 1, NY - 2)

    sp32[0:8, :] = jnp.zeros((8, 1408), F32)
    for c in range(3):
        v = spec_ref[c].astype(F32)
        last = jnp.broadcast_to(v[:, 1280:1281], (PD, 128))
        for p0, n, r0, rows, lead in CHUNKS:
            r = r0 + lead + c * n
            sp32[r : r + n, 0:1280] = v[p0 : p0 + n, 0:1280]
            sp32[r : r + n, 1280:1408] = last[p0 : p0 + n, :]
    tail = jnp.transpose(sp32[:, 1280:1408], (1, 0))[0:8, :]
    lane = lax.broadcasted_iota(jnp.int32, (8, 128), 1)
    sub = lax.broadcasted_iota(jnp.int32, (8, 896), 0)
    extra = jnp.zeros((8, 896), F32)
    for ch, (p0, n, r0, rows, lead) in enumerate(CHUNKS):
        part = jnp.where((lane >= r0 + lead) & (lane < r0 + rows), tail, 0.0)
        part = jnp.concatenate([part, jnp.zeros((8, 768), F32)], axis=1)
        part = pltpu.roll(part, lax.rem(y * rows - r0 + 896, 896), 1)
        part = jnp.broadcast_to(part[0:1, :], (8, 896))
        extra = jnp.where(sub == ch, part, extra)
    sp32[0:8, 0:768] = extra[:, 0:768]

    def cast_own(i, c):
        r = pl.multiple_of(i * 16, 16)
        gath[y, pl.ds(r, 16), :] = sp32[pl.ds(r, 16), 0:1280].astype(BF16)
        return c
    lax.fori_loop(0, 8, cast_own, 0)

    count = 15 + 3
    count += jnp.where(y < NY - 1, 3, 0) + jnp.where(y > 0, 3, 0)
    count += jnp.where(jnp.logical_and(w == NW - 1, y < NY - 2), 2, 0)
    count += jnp.where(jnp.logical_and(w == 0, y > 1), 2, 0)
    count += jnp.where(jnp.logical_and(w == 0, y == 1), 14, 0)
    count += jnp.where(jnp.logical_and(w == NW - 1, y == NY - 2), 14, 0)
    pl.semaphore_wait(barrier, count)

    def block(origin, piece, half):
        ch, l0, ln = PIECES[piece]
        _, _, r0, rows, _ = CHUNKS[ch]
        if half == 0:
            ln = ln // 2
        elif half == 1:
            l0, ln = l0 + ln // 2, ln // 2
        return gath.at[origin, pl.ds(r0, rows), pl.ds(l0, ln)]

    def ring(origin, piece, step, upward):
        half = None if step < 3 else (0 if upward else 1)
        ref = block(origin, piece, half)
        s, r = (up_s, up_r) if upward else (dn_s, dn_r)
        return pltpu.make_async_remote_copy(
            src_ref=ref, dst_ref=ref, send_sem=s.at[piece, step], recv_sem=r.at[piece, step],
            device_id=dev(w, up_y if upward else dn_y), device_id_type=MESH)

    def to_sib(origin, piece, idx, half=None):
        ref = block(origin, piece, half)
        return pltpu.make_async_remote_copy(
            src_ref=ref, dst_ref=ref, send_sem=sib_s.at[piece, idx], recv_sem=sib_r.at[piece, idx],
            device_id=dev(w, sib_y), device_id_type=MESH)

    def origin_of(step, upward):
        return lax.rem(y + NY - 2 * step, NY) if upward else lax.rem(y + 2 * step, NY)

    def send_own(piece):
        ring(y, piece, 0, True).start()
        ring(y, piece, 0, False).start()
        to_sib(y, piece, 0).start()

    def ring_step(piece, step):
        for upward in (True, False):
            org = origin_of(step, upward)
            ring(org, piece, step - 1, upward).wait_recv()
            if step < 4:
                ring(org, piece, step, upward).start()
                to_sib(org, piece, 2 * step - (1 if upward else 0)).start()
            else:
                to_sib(org, piece, 7 if upward else 8, 0 if upward else 1).start()

    def sib_wait(piece):
        base = sib_y
        to_sib(base, piece, 0).wait_recv()
        for step in range(1, 5):
            for upward in (True, False):
                org = lax.rem(base + NY - 2 * step, NY) if upward else lax.rem(base + 2 * step, NY)
                if step < 4:
                    to_sib(org, piece, 2 * step - (1 if upward else 0)).wait_recv()
                else:
                    to_sib(org, piece, 7 if upward else 8, 0 if upward else 1).wait_recv()

    def sends_done(piece):
        for step in range(4):
            for upward in (True, False):
                ring(y, piece, step, upward).wait_send()
        for idx in range(7):
            to_sib(y, piece, idx).wait_send()
        to_sib(y, piece, 7, 0).wait_send()
        to_sib(y, piece, 8, 1).wait_send()

    anchor = anchor_ref[0].astype(F32)

    def leg_rows(ch):
        p0, n, _, _, _ = CHUNKS[ch]
        pos = lax.broadcasted_iota(jnp.int32, (1, 1280), 1)
        lane16 = lax.broadcasted_iota(jnp.int32, (1, 256), 1) % 16

        def one(p, c):
            limit = TRUNC - (w * PD + p0 + p)
            low = jnp.where(pos < limit, 1.0, 0.0)
            rows = leg_ref[p0 + p]
            tile = rows[:, 0:1280].astype(F32)
            a = pl.multiple_of(p * 16, 16)
            b = pl.multiple_of(n * 16 + p * 16, 16)
            leg2[ch % 2, pl.ds(a, 16), :] = (tile * low).astype(BF16)
            leg2[ch % 2, pl.ds(b, 16), :] = (tile * (1.0 - low)).astype(BF16)
            last = rows[:, 1280:1281].astype(F32)
            legx[ch % 2, pl.ds(a, 16), :] = jnp.zeros((16, 256), BF16)
            legx[ch % 2, pl.ds(b, 16), :] = jnp.where(lane16 == ch, last, 0.0).astype(BF16)
            return c
        lax.fori_loop(0, n, one, 0)

    def fourier(ch):
        p0, n, r0, rows, lead = CHUNKS[ch]
        m = 2 * n * 16
        mask, fold = (mask_a, fold_a) if ch == 0 else (mask_b, fold_b)
        for nb in range(2):
            g = gath[8 * nb : 8 * nb + 8, r0 : r0 + rows, :].reshape(8 * rows, 1280)
            x = gath[:, 0:16, 8 * rows * nb : 8 * rows * (nb + 1)].reshape(256, 8 * rows)

            def blockm(i, c):
                a = pl.multiple_of(i * MB, MB)
                res = dot_nt(leg2[ch % 2, pl.ds(a, MB), :], g)
                res = res + dot_nn(legx[ch % 2, pl.ds(a, MB), :], x)
                hi, lo = split2(res * mask[pl.ds(a, MB), :].astype(F32))
                part = dot_nn(hi, fold[nb, 0]) + dot_nn(lo, fold[nb, 1])
                part = part.reshape(MB // 16, 16, 128)
                t = pl.ds(pl.multiple_of(i * (MB // 16), MB // 16), MB // 16)
                if nb == 0:
                    fs[t] = part
                else:
                    fs[t] = fs[t] + part
                return c
            lax.fori_loop(0, m // MB, blockm, 0)
        f0 = (0, 16, 48)[ch]
        for l in range(16):
            v = fs[0 : 2 * n, l, :].astype(BF16)
            fsend[l, f0 : f0 + 2 * n, :] = v

    def wave_copy(ch, o):
        n = CHUNKS[ch][1]
        f0 = (0, 16, 48)[ch]
        to = lax.rem(w + o, NW)
        return pltpu.make_async_remote_copy(
            src_ref=fsend.at[to, pl.ds(f0, 2 * n), :], dst_ref=frecv.at[ch, w, pl.ds(0, 2 * n), :],
            send_sem=fa_s.at[ch, o], recv_sem=fa_r.at[ch, o],
            device_id=dev(to, y), device_id_type=MESH)

    def wave_send(ch):
        n = CHUNKS[ch][1]
        f0 = (0, 16, 48)[ch]
        lax.fori_loop(1, NW, lambda o, c: (wave_copy(ch, o).start(), c)[1], 0)
        frecv[ch, w, 0 : 2 * n, :] = fsend[w, f0 : f0 + 2 * n, :]

    def wave_recv(ch):
        lax.fori_loop(1, NW, lambda o, c: (wave_copy(ch, o).wait_recv(), c)[1], 0)

    def wave_done(ch):
        lax.fori_loop(1, NW, lambda o, c: (wave_copy(ch, o).wait_send(), c)[1], 0)

    def table(ch):
        p0, n, _, _, _ = CHUNKS[ch]
        k0 = KOFF[ch]
        shift = 4 if n == 16 else 3

        def one(t, c):
            q = t * 128 + lax.broadcasted_iota(jnp.int32, (1, 128), 1)
            ww = q >> (shift + 1)
            h = (q >> shift) & 1
            pg = ww * PD + p0 + (q & (n - 1))
            mi = jnp.where(h == 0, pg, TRUNC - 1 - pg)
            m = mi.astype(F32)
            s = jnp.where(mi == 0, 1.0, 2.0)

            def angle(x):
                return (x - NLON * jnp.floor(x * (1.0 / NLON))) * (2.0 * math.pi / NLON)

            d = lax.broadcasted_iota(jnp.int32, (LON, 128), 0).astype(F32)
            fine = angle(m * d)
            cf, sf = jnp.cos(fine) * s, jnp.sin(fine) * s
            b = lax.broadcasted_iota(jnp.int32, (16, 128), 0).astype(F32) * LON
            coarse = angle(m * (anchor + b))
            cc, sc = jnp.cos(coarse), jnp.sin(coarse)
            col = pl.multiple_of(k0 + t * 128, 128)
            for i in range(16):
                ci, si = cc[i : i + 1, :], sc[i : i + 1, :]
                vc = ci * cf - si * sf
                vs = -(si * cf + ci * sf)
                hi, lo = split2(vc)
                tcos[0, LON * i : LON * i + LON, pl.ds(col, 128)] = hi
                tcos[1, LON * i : LON * i + LON, pl.ds(col, 128)] = lo
                hi, lo = split2(vs)
                tsin[0, LON * i : LON * i + LON, pl.ds(col, 128)] = hi
                tsin[1, LON * i : LON * i + LON, pl.ds(col, 128)] = lo
            return c
        lax.fori_loop(0, 2 * n * 16 // 128, one, 0)

    def contract(ch):
        n = CHUNKS[ch][1]
        k0, k = KOFF[ch], 2 * n * 16
        f = frecv[ch, :, 0 : 2 * n, :].reshape(k, 128)

        def one(i, c):
            a = pl.multiple_of(i * 128, 128)
            for tab, acc in ((tcos, acc_c), (tsin, acc_s)):
                v = dot_nn(tab[0, pl.ds(a, 128), k0 : k0 + k], f)
                v = v + dot_nn(tab[1, pl.ds(a, 128), k0 : k0 + k], f)
                if ch == 0:
                    acc[pl.ds(a, 128), :] = v
                else:
                    acc[pl.ds(a, 128), :] = acc[pl.ds(a, 128), :] + v
            return c
        lax.fori_loop(0, 4, one, 0)

    lane_h = lax.broadcasted_iota(jnp.int32, (128, 128), 1)

    def nest_copy(i):
        if i < 4:
            src, dst = (cpk_s, cpk_r) if i < 2 else (rpk_s, rpk_r)
            src, dst = src.at[i % 2], dst.at[i % 2]
        else:
            src, dst = info_s, info_r.at[i - 4]
        to = (dev(lax.rem(w + NW - 1, NW), y), dev(lax.rem(w + 1, NW), y), dev(w, near(-1)), dev(w, near(1)))[i % 4]
        return pltpu.make_async_remote_copy(
            src_ref=src, dst_ref=dst, send_sem=nest_s.at[i], recv_sem=nest_r.at[i],
            device_id=to, device_id_type=MESH)

    can_send = (w > 0, w < NW - 1, y > 0, y < NY - 1)
    can_recv = (w < NW - 1, w > 0, y < NY - 1, y > 0)

    def nest_do(which, cond, go):
        for i in which:
            @pl.when(cond[i % 4])
            def _(i=i):
                go(nest_copy(i))

    def nest_pack():
        info_s[...] = jnp.zeros((8, 128), F32)
        info_s[0:1, :] = ridx_ref[...].astype(F32)
        info_s[1:2, :] = rwt_ref[...]
        info_s[2:3, :] = cidx_ref[...].astype(F32)
        info_s[3:4, :] = cwt_ref[...]
        left = jnp.zeros((128, 128), F32)
        right = jnp.zeros((128, 128), F32)
        for k in range(KF):
            v = nest_ref[k].astype(F32)
            here = (lane_h >= 4 * k) & (lane_h < 4 * k + 4)
            left = jnp.where(here, pltpu.roll(v, 4 * k, 1) if k else v, left)
            right = jnp.where(here, pltpu.roll(v, 4 * k + 4, 1), right)
        cpk_s[0] = left.astype(BF16)
        cpk_s[1] = right.astype(BF16)
        row = (lax.broadcasted_iota(jnp.int32, (EXT, 256), 0) + (128 * y - 8)).astype(F32)
        j = lax.broadcasted_iota(jnp.int32, (EXT, 256), 1)
        col = (jnp.where(j < 192, j, j - 256) + 128 * w).astype(F32)
        keep, _ = shares(row, col, zone_ref)
        damp[...] = keep * DIFFUSION
        nest_do((0, 1, 4, 5, 6, 7), can_send, lambda c: c.start())

    def nest_cols():
        nest_do((0, 1), can_recv, lambda c: c.wait_recv())
        from_right = cpk_r[0].astype(F32)
        from_left = cpk_r[1].astype(F32)

        def one(k, c):
            a = pltpu.roll(from_right, lax.rem(128 - 4 * k, 128), 1)
            b = pltpu.roll(from_left, lax.rem(252 - 4 * k, 128), 1)
            e = jnp.where(lane_h < 4, a, jnp.where(lane_h >= 124, b, 0.0))
            ext[k, 0:8, :] = jnp.zeros((8, 256), F32)
            ext[k, 136:144, :] = jnp.zeros((8, 256), F32)
            ext[k, 8:136, 0:128] = nest_ref[k].astype(F32)
            ext[k, 8:136, 128:256] = e
            return c
        lax.fori_loop(0, KF, one, 0)
        for i, r in ((0, 8), (1, 132)):
            for k in range(KF):
                rpk[4 * k : 4 * k + 4, :] = ext[k, r : r + 4, :]
            rpk_s[i] = rpk[...].astype(BF16)
        nest_do((2, 3), can_send, lambda c: c.start())

    def nest_rows():
        nest_do((2, 3), can_recv, lambda c: c.wait_recv())
        for i, r in ((0, 136), (1, 4)):
            rpk[...] = rpk_r[i].astype(F32)
            for k in range(KF):
                ext[k, r : r + 4, :] = rpk[4 * k : 4 * k + 4, :]

    def nest_sweeps(k0, k1_):
        def one(k, c):
            x = ext[k]
            for _ in range(NSWEEP):
                t = x + pltpu.roll(x, 1, 0) + pltpu.roll(x, EXT - 1, 0)
                t = t + pltpu.roll(x, 1, 1) + pltpu.roll(x, 255, 1)
                x = t * damp[...]
            field_out[k] = x[8:136, 0:128]
            return c
        lax.fori_loop(k0, k1_, one, 0)

    def nest_done():
        nest_do((4, 5, 6, 7), can_recv, lambda c: c.wait_recv())
        nest_do(range(8), can_send, lambda c: c.wait_send())
        info_out[0] = info_s[...]
        info_out[1:5] = info_r[...]

    send_own(0)
    send_own(1)
    nest_pack()
    ring_step(0, 1)
    send_own(2)
    table(0)
    table(1)
    leg_rows(0)
    nest_cols()
    ring_step(0, 2)
    ring_step(1, 1)
    table(2)
    nest_rows()
    leg_rows(1)
    ring_step(0, 3)
    ring_step(2, 1)
    nest_sweeps(0, 8)
    ring_step(1, 2)
    ring_step(0, 4)
    sib_wait(0)
    fourier(0)
    wave_send(0)
    ring_step(2, 2)
    nest_sweeps(8, 16)
    ring_step(1, 3)
    wave_recv(0)
    contract(0)
    ring_step(2, 3)
    nest_sweeps(16, KF)
    nest_done()
    ring_step(1, 4)
    sib_wait(1)
    leg_rows(2)
    fourier(1)
    wave_send(1)
    ring_step(2, 4)
    sib_wait(2)
    fourier(2)
    wave_send(2)
    wave_recv(1)
    contract(1)
    wave_recv(2)
    contract(2)

    prow[:, 0:128] = jnp.zeros((KF, 128), F32)
    prow[:, 512:640] = jnp.zeros((KF, 128), F32)
    for i in range(4):
        tc = jnp.transpose(acc_c[128 * i : 128 * i + 128, :], (1, 0))
        ts = jnp.transpose(acc_s[128 * i : 128 * i + 128, :], (1, 0))
        val = tc[0:24] + tc[48:72] + ts[24:48] + ts[72:96]
        prow[:, 48 + 128 * i : 176 + 128 * i] = val
    for v in range(NW):
        psend[v] = prow[:, LON * v : LON * v + WIN]

    def win(src, to_w, to_y, slot, sem):
        return pltpu.make_async_remote_copy(
            src_ref=psend.at[src], dst_ref=pbuf.at[slot], send_sem=w_s.at[sem], recv_sem=w_r.at[slot],
            device_id=dev(to_w, to_y), device_id_type=MESH)

    def edges(go):
        @pl.when(y < NY - 1)
        def _():
            go(0, 0, near(1), 1 + w, 16)
            go(NW - 1, NW - 1, near(1), 1 + w, 17)

        @pl.when(y > 0)
        def _():
            go(0, 0, near(-1), 33 + w, 18)
            go(NW - 1, NW - 1, near(-1), 33 + w, 19)

        @pl.when(jnp.logical_and(w == NW - 1, y < NY - 2))
        def _():
            go(0, 0, near(2), 0, 20)
            go(NW - 1, NW - 1, near(2), 0, 21)

        @pl.when(jnp.logical_and(w == 0, y > 1))
        def _():
            go(0, 0, near(-2), 49, 22)
            go(NW - 1, NW - 1, near(-2), 49, 23)

        @pl.when(jnp.logical_and(w == 0, y == 1))
        def _():
            lax.fori_loop(1, NW - 1, lambda v, c: (go(v, v, near(-1), 33 + w, 24 + v), c)[1], 0)

        @pl.when(jnp.logical_and(w == NW - 1, y == NY - 2))
        def _():
            lax.fori_loop(1, NW - 1, lambda v, c: (go(v, v, near(1), 1 + w, 24 + v), c)[1], 0)

    def own_win(o):
        to = lax.rem(w + o, NW)
        return win(to, to, y, 17 + w, o)

    lax.fori_loop(1, NW, lambda o, c: (own_win(o).start(), c)[1], 0)
    edges(lambda *a: win(*a).start())
    pbuf[17 + w] = psend[w]

    for ch in range(3):
        wave_done(ch)
    for piece in range(len(PIECES)):
        sends_done(piece)

    def got(slot):
        win(0, w, sib_y, slot, 0).wait_recv()

    lax.fori_loop(1, NW, lambda o, c: (got(17 + lax.rem(w + o, NW)), c)[1], 0)

    @pl.when(jnp.logical_and(wedge, y > 0))
    def _():
        lax.fori_loop(0, NW, lambda o, c: (got(1 + o), c)[1], 0)

    @pl.when(jnp.logical_and(wedge, y < NY - 1))
    def _():
        lax.fori_loop(0, NW, lambda o, c: (got(33 + o), c)[1], 0)

    @pl.when(jnp.logical_and(wedge, y > 1))
    def _():
        got(0)

    @pl.when(jnp.logical_and(wedge, y < NY - 2))
    def _():
        got(49)

    @pl.when(jnp.logical_and(jnp.logical_not(wedge), y == 0))
    def _():
        got(33)

    @pl.when(jnp.logical_and(jnp.logical_not(wedge), y == NY - 1))
    def _():
        got(16)

    def copy_out(i, c):
        win_out[i] = pbuf[i]
        return c
    lax.fori_loop(0, SLOTS, copy_out, 0)
    lax.fori_loop(1, NW, lambda o, c: (own_win(o).wait_send(), c)[1], 0)
    edges(lambda *a: win(*a).wait_send())


def vmem_spec():
    return pl.BlockSpec(memory_space=pltpu.VMEM)


def spectral(spectra, legendre, lon_anchor, zone_width, nest_state, ridx, rwt, cidx, cwt):
    spec = jnp.transpose(spectra, (1, 0, 2))
    (mask_a, fold_a), (mask_b, fold_b), _ = chunk_consts()
    np_ = len(PIECES)
    smem = pl.BlockSpec(memory_space=pltpu.SMEM)
    dma = pltpu.SemaphoreType.DMA
    return pl.pallas_call(
        k1,
        out_shape=(
            jax.ShapeDtypeStruct((SLOTS, KF, WIN), F32),
            jax.ShapeDtypeStruct((KF, 128, 128), F32),
            jax.ShapeDtypeStruct((5, 8, 128), F32),
        ),
        in_specs=[smem, smem] + [vmem_spec()] * 11,
        out_specs=(vmem_spec(), vmem_spec(), vmem_spec()),
        scratch_shapes=[
            pltpu.VMEM((NY, 128, 1280), BF16),
            pltpu.VMEM((128, 1408), F32),
            pltpu.VMEM((2, 512, 1280), BF16),
            pltpu.VMEM((2, 512, 256), BF16),
            pltpu.VMEM((32, 16, 128), F32),
            pltpu.VMEM((16, 80, 128), BF16),
            pltpu.VMEM((3, 16, 32, 128), BF16),
            pltpu.VMEM((2, NLB, NKEY), BF16),
            pltpu.VMEM((2, NLB, NKEY), BF16),
            pltpu.VMEM((NLB, 128), F32),
            pltpu.VMEM((NLB, 128), F32),
            pltpu.VMEM((16, KF, WIN), F32),
            pltpu.VMEM((KF, 640), F32),
            pltpu.VMEM((SLOTS, KF, WIN), F32),
            pltpu.VMEM((KF, EXT, 256), F32),
            pltpu.VMEM((EXT, 256), F32),
            pltpu.VMEM((2, 128, 128), BF16),
            pltpu.VMEM((2, 128, 128), BF16),
            pltpu.VMEM((96, 256), F32),
            pltpu.VMEM((2, 96, 256), BF16),
            pltpu.VMEM((2, 96, 256), BF16),
            pltpu.VMEM((8, 128), F32),
            pltpu.VMEM((4, 8, 128), F32),
            dma((8,)), dma((8,)),
            dma((np_, 4)), dma((np_, 4)),
            dma((np_, 4)), dma((np_, 4)),
            dma((np_, 9)), dma((np_, 9)),
            dma((3, 16)), dma((3, 16)),
            dma((40,)), dma((SLOTS,)),
        ],
        compiler_params=pltpu.CompilerParams(
            collective_id=0, has_side_effects=True, vmem_limit_bytes=60 * 1024 * 1024),
    )(lon_anchor, zone_width, spec, legendre,
      jnp.asarray(mask_a, BF16), jnp.asarray(mask_b, BF16),
      jnp.asarray(fold_a, BF16), jnp.asarray(fold_b, BF16),
      nest_state, ridx, rwt, cidx, cwt)


def dot3(a, b):
    ah, al = split2(a)
    bh, bl = split2(b)
    return dot_nn(ah, bh) + dot_nn(ah, bl) + dot_nn(al, bh)


def pick(axis_iota, index, weight):
    return jnp.where(axis_iota == index, 1.0 - weight, 0.0) + jnp.where(
        axis_iota == index + 1.0, weight, 0.0
    )


def fiota(shape, axis):
    return lax.broadcasted_iota(jnp.int32, shape, axis).astype(F32)


def k2(zone_ref, win_ref, field_ref, info_ref, band_out, nest_out, acc, xs, tau):
    w = lax.axis_index("wave")
    y = lax.axis_index("ny")

    def band(k, c):
        v = win_ref[17:33, k, :]
        band_out[k] = pltpu.roll(v, 80, 1)[:, 0:LON]
        return c
    lax.fori_loop(0, KF, band, 0)

    def base(k, c):
        acc[k] = field_ref[k]
        return c
    lax.fori_loop(0, KF, base, 0)

    own, right, left, below, above = (info_ref[i] for i in range(5))
    turned = [jnp.transpose(jnp.concatenate([v, jnp.zeros((120, 128), F32)], 0), (1, 0))
              for v in (own, below, above)]
    lon0 = (w * LON - 48).astype(F32)
    lat0 = (y * 16 - 17).astype(F32)

    @pl.when(jnp.logical_or(y == 0, y == NY - 1))
    def _():
        first = jnp.where(y == 0, 0, 104)
        lane = lax.broadcasted_iota(jnp.int32, (1, 128), 1)
        far_i = jnp.where(lane < 4, right[2:3], jnp.where(lane >= 124, left[2:3], -4096.0))
        far_w = jnp.where(lane < 4, right[3:4], left[3:4])
        cidx = jnp.concatenate([own[2:3], far_i], 1) - lon0
        cwt = jnp.concatenate([own[3:4], far_w], 1)
        cmat = pick(fiota((128, 256), 0), cidx, cwt)

        def cross(i, c):
            xs[i] = dot3(win_ref[16 + i], cmat)
            return c
        lax.fori_loop(0, 18, cross, 0)

        cols = jnp.where(y == 0, turned[0][0:24, :], turned[0][104:128, :])
        ridx = cols[:, 0:1] - lat0 - 16.0
        rwt = cols[:, 1:2]
        row = fiota((24, 256), 0) + (128 * y + first).astype(F32)
        j = lax.broadcasted_iota(jnp.int32, (24, 256), 1)
        col = (jnp.where(j < 192, j, j - 256) + 128 * w).astype(F32)
        keep, share = shares(row, col, zone_ref)
        keep = keep * DIFFUSION
        keep = jnp.where((row < 20.0) | (row >= 2028.0), keep, 0.0)
        share = jnp.where((row < 16.0) | (row >= 2032.0), share, 0.0)
        blend = [jnp.broadcast_to(pick(float(i), ridx, rwt), (24, 256)) for i in range(18)]

        def level(k, c):
            t = jnp.zeros((24, 256), F32)
            for i in range(18):
                t = t + blend[i] * xs[i, pl.ds(k, 1), :]
            q = share * t
            g = q
            for _ in range(NSWEEP - 1):
                v = g + pltpu.roll(g, 1, 0) + pltpu.roll(g, 23, 0)
                v = v + pltpu.roll(g, 1, 1) + pltpu.roll(g, 255, 1)
                g = v * keep + q
            at = pl.ds(pl.multiple_of(first, 8), 24)
            acc[k, at, :] = acc[k, at, :] + g[:, 0:128]
            return c
        lax.fori_loop(0, KF, level, 0)

    @pl.when(jnp.logical_or(w == 0, w == NW - 1))
    def _():
        cbase = jnp.where(w == 0, 0, 96)
        lane = lax.broadcasted_iota(jnp.int32, (1, 128), 1)
        vec = jnp.concatenate([own[2:4] - jnp.where(fiota((2, 128), 0) == 0.0, lon0, 0.0),
                               jnp.zeros((6, 128), F32)], 0)
        vec = jnp.where(w == 0, vec, pltpu.roll(vec, 32, 1))
        mats = []
        for i in range(4):
            v = pltpu.roll(vec, LON * i, 1) if i else vec
            here = (lane >= LON * i) & (lane < LON * i + LON)
            mats.append(jnp.where(here, pick(fiota((128, 128), 0), v[0:1], v[1:2]), 0.0))
        cmat = jnp.concatenate(mats, 0)
        rows = jnp.concatenate([turned[2][120:128], turned[0], turned[1][0:8]], 0)
        rmat = pick(fiota((EXT, SLOTS), 1), rows[:, 0:1] - lat0, rows[:, 1:2])

        row = fiota((EXT, 128), 0) + (128 * y - 8).astype(F32)
        inner = lax.broadcasted_iota(jnp.int32, (EXT, 128), 1) % LON
        col = (inner + cbase + 128 * w).astype(F32)
        keep, share = shares(row, col, zone_ref)
        keep = keep * DIFFUSION
        share = jnp.where((col < 16.0) | (col >= 2032.0), share, 0.0)
        share = jnp.where((row >= 16.0) & (row < 2032.0), share, 0.0)
        not_first = jnp.where(inner == 0, 0.0, 1.0)
        not_last = jnp.where(inner == LON - 1, 0.0, 1.0)
        lane_h = lax.broadcasted_iota(jnp.int32, (128, 128), 1)
        strip = (lane_h >= cbase) & (lane_h < cbase + LON)

        def group(t, c):
            p = jnp.concatenate([win_ref[:, 4 * t + i, :] for i in range(4)], 1)
            q = share * dot3(rmat, dot3(p, cmat))
            g = q
            for _ in range(NSWEEP - 1):
                v = g + pltpu.roll(g, 1, 0) + pltpu.roll(g, EXT - 1, 0)
                v = v + pltpu.roll(g, 1, 1) * not_first + pltpu.roll(g, 127, 1) * not_last
                g = v * keep + q
            g = g[8:136, :]
            for i in range(4):
                part = pltpu.roll(g, lax.rem(cbase + 128 - LON * i, 128), 1)
                acc[4 * t + i] = acc[4 * t + i] + jnp.where(strip, part, 0.0)
            return c
        lax.fori_loop(0, KF // 4, group, 0)

    def last(k, c):
        nest_out[k] = acc[k].astype(BF16)
        return c
    lax.fori_loop(0, KF, last, 0)


def relax(zone_width, windows, field, info):
    return pl.pallas_call(
        k2,
        out_shape=(
            jax.ShapeDtypeStruct((KF, 16, LON), F32),
            jax.ShapeDtypeStruct((KF, 128, 128), BF16),
        ),
        in_specs=[pl.BlockSpec(memory_space=pltpu.SMEM)] + [vmem_spec()] * 3,
        out_specs=(vmem_spec(), vmem_spec()),
        scratch_shapes=[
            pltpu.VMEM((KF, 128, 128), F32),
            pltpu.VMEM((18, KF, 256), F32),
            pltpu.VMEM((8, 128), F32),
        ],
        compiler_params=pltpu.CompilerParams(vmem_limit_bytes=40 * 1024 * 1024),
    )(zone_width, windows, field, info)


def body(
    spectra, legendre, lon_anchor, row_index, row_weight, col_index, col_weight, zone_width,
    nest_state,
):
    windows, field, info = spectral(
        spectra, legendre, lon_anchor, zone_width, nest_state,
        row_index.reshape(1, 128), row_weight.reshape(1, 128),
        col_index.reshape(1, 128), col_weight.reshape(1, 128),
    )
    return relax(zone_width, windows, field, info)


def solution(mesh):
    placed = (
        P("wave", "ny", None), P("wave", "ny", None), P(), P("ny"), P("ny"), P("wave"), P("wave"),
        P(), P(None, "ny", "wave"),
    )
    return jax.shard_map(
        body, mesh=mesh, in_specs=placed,
        out_specs=(P(None, "ny", "wave"), P(None, "ny", "wave")), check_vma=False,
    )
```

profile of v0, /device:TPU:0, one launch (start us, length us, event | category | flops | bytes accessed | tf_op | source)
XLA Modules:
  0.0 94.8 jit_solution(296132764206570980)
XLA Ops:
  1.3 0.0 copy-start.3
  1.3 71.3 %shard_map.140 = (f32[56,24,128]{2,1,0:T(8,128)}, f32[24,128,128]{2,1,0:T(8,128)}, f32[5,8,128]{2,1,0:T(8,128)}) custom-call(s32[1]{0:T(128)S(6)} %copy.15.anchor_ref, s32[4]{0:T(128)} %zone_ref.3, bf16[3,40,1281]{2,1,0:T(8,128)(2,1)} %bitcast.5, bf16[40,16,1281]{2,1,0:T(8,128)(2,1)} %leg_ref.1, bf16[256,256]{1,0:T(8,128)(2,1)} %constant.8.clone.mask_a, ...), custom_call_target="tpu_custom_call" | custom-call | tf_op jit(solution)/shard_map/pallas_call | solution.py:614
  72.6 0.0 copy-done.3
  72.6 0.0 copy-start
  72.6 1.4 %copy-done = f32[24,128,128]{2,1,0:T(8,128)S(1)} copy-done((f32[24,128,128]{2,1,0:T(8,128)S(1)}, f32[24,128,128]{2,1,0:T(8,128)}, u32[]{:S(2)}) %copy-start) | copy-done | bytes 1572888
  74.0 0.0 copy-start.1
  74.0 1.1 %copy-done.1 = f32[56,24,128]{2,1,0:T(8,128)S(1)} copy-done((f32[56,24,128]{2,1,0:T(8,128)S(1)}, f32[56,24,128]{2,1,0:T(8,128)}, u32[]{:S(2)}) %copy-start.1) | copy-done | bytes 688152
  75.1 0.0 copy-start.2
  75.1 0.7 copy-done.2
  75.9 18.9 %shard_map.141 = (f32[24,16,32]{2,1,0:T(8,128)}, bf16[24,128,128]{2,1,0:T(8,128)(2,1)}) custom-call(s32[4]{0:T(128)S(1)} %copy-done.3, f32[56,24,128]{2,1,0:T(8,128)S(1)} %copy-done.1, f32[24,128,128]{2,1,0:T(8,128)S(1)} %copy-done, f32[5,8,128]{2,1,0:T(8,128)S(1)} %copy-done.2), custom_call_target="tpu_custom_call" | custom-call | tf_op jit(solution)/shard_map/pallas_call | solution.py:791
Async XLA Ops:
  1.3 71.3 %copy-start.3 = (s32[4]{0:T(128)S(1)}, s32[4]{0:T(128)}, u32[]{:S(2)}) copy-start(s32[4]{0:T(128)} %zone_ref.3) | copy-start | bytes 52
  72.6 1.4 %copy-start = (f32[24,128,128]{2,1,0:T(8,128)S(1)}, f32[24,128,128]{2,1,0:T(8,128)}, u32[]{:S(2)}) copy-start(f32[24,128,128]{2,1,0:T(8,128)} %get-tuple-element.6.field_ref) | copy-start | bytes 4718596
  74.0 1.1 %copy-start.1 = (f32[56,24,128]{2,1,0:T(8,128)S(1)}, f32[56,24,128]{2,1,0:T(8,128)}, u32[]{:S(2)}) copy-start(f32[56,24,128]{2,1,0:T(8,128)} %get-tuple-element.5.win_ref) | copy-start | bytes 2064388
  75.1 0.7 copy-start.2
where the time goes:
time: 95 us; the launch traced here: 94.8 us
  Pallas kernels  90.2 us (95%)
  local copies, waits for them, and re-layouts  3.23 us (3%)
  between operations  1.31 us (1%)
    pallas_call x1, Pallas kernels, spectral(): pl.pallas_call(k1, out_shape=(jax.ShapeDtypeStruct((SLOTS, KF, WIN), F32)...  71.3 us
    pallas_call x1, Pallas kernels, relax(): pl.pallas_call(k2, out_shape=(jax.ShapeDtypeStruct((KF, 16, LON), F32), j...  18.9 us
    unnamed x8, local copies, waits for them, and re-layouts  3.23 us

commit v1 on v0

v1 whole, which is shorter than its diff:
```python
import functools
import math

import jax
import jax.numpy as jnp
import numpy as np
from jax import lax
from jax.experimental import pallas as pl
from jax.experimental.pallas import tpu as pltpu
from jax.sharding import PartitionSpec as P

MESH = pl.DeviceIdType.MESH
NW = 16
NY = 16
PD = 40
TRUNC = 1280
NLON = 5120
LON = 32
KF = 24
NLB = 512
NSWEEP = 4
DIFFUSION = 0.2
F32 = jnp.float32
BF16 = jnp.bfloat16
CHUNKS = ((0, 8, 0, 32, 8), (8, 16, 32, 48, 0), (24, 16, 80, 48, 0))
HALVES = (((0, 16), (16, 16)), ((0, 48), (0, 0)), ((0, 0), (0, 48)))
KOFF = (0, 256, 768)
NKEY = 1280
SLOTS = 24
EXT = 144
WIN = 128


def lane_of(chan):
    return 16 * (chan % 8) + chan // 8


def first_consts():
    _, n, _, rows, lead = CHUNKS[0]
    row = np.arange(2 * n * 16)
    col = np.arange(16 * rows)
    inner = col % rows - lead
    cpair = np.where(inner >= 0, inner % n, -1)
    mask = ((row // 16) % n)[:, None] == cpair[None, :]
    fold = np.zeros((2, 16 * rows, 128), np.float32)
    for i in range(16 * rows):
        if inner[i] >= 0:
            lane = lane_of((i // rows) * 3 + inner[i] // n)
            fold[0, i, lane] = 1.0
            fold[1, i, lane + 8] = 1.0
    return mask.astype(np.float32), fold


def split2(x):
    hi = x.astype(BF16)
    lo = (x - hi.astype(F32)).astype(BF16)
    return hi, lo


def dot_nt(a, b):
    return lax.dot_general(a, b, (((1,), (1,)), ((), ())), preferred_element_type=F32)


def dot_nn(a, b):
    return lax.dot_general(a, b, (((1,), (0,)), ((), ())), preferred_element_type=F32)


def ramps(pos, first, last, total):
    return jnp.maximum(
        jnp.maximum(0.0, 1.0 - pos / first), jnp.maximum(0.0, 1.0 - (total - 1 - pos) / last)
    )


def shares(row, col, zone_ref):
    z = [zone_ref[i].astype(F32) for i in range(4)]
    share = jnp.maximum(ramps(row, z[0], z[1], 2048.0), ramps(col, z[2], z[3], 2048.0))
    inside = (row >= 0.0) & (row < 2048.0) & (col >= 0.0) & (col < 2048.0)
    inside = jnp.where(inside, 1.0, 0.0)
    return (1.0 - share) * inside, share * inside


def dot3(a, bh, bl):
    ah, al = split2(a)
    return dot_nn(ah, bh) + dot_nn(ah, bl) + dot_nn(al, bh)


def pick(axis_iota, index, weight):
    return jnp.where(axis_iota == index, 1.0 - weight, 0.0) + jnp.where(
        axis_iota == index + 1.0, weight, 0.0
    )


def fiota(shape, axis):
    return lax.broadcasted_iota(jnp.int32, shape, axis).astype(F32)


def k1(
    anchor_ref, zone_ref, spec_ref, ridx_ref, rwt_ref, cidx_ref, cwt_ref,
    leg_hbm, mask_hbm, fold_hbm, nest_hbm,
    band_out, nest_out,
    leg_ref, mask_ref, fold_ref, nest_ref, load_s,
    gath, sp32, leg2, legx, fs, fsend, frecv, tcos, tsin, acc_c, acc_s, turn, psend, prow, pbuf,
    ext, damp, cpk_s, cpk_r, rpk, rpk_s, rpk_r, info_s, info_r, nest_s, nest_r,
    field, row_mats, row_part, row_blend, row_x, col_mats, col_part, col_blend, col_p, col_q,
    q_out, q_in, q_s, q_r,
    up_s, up_r, dn_s, dn_r, sib_s, sib_r, fa_s, fa_r, w_s, w_r,
):
    w = lax.axis_index("wave")
    y = lax.axis_index("ny")
    wedge = jnp.logical_or(w == 0, w == NW - 1)

    def near(d):
        return lax.rem(y + (NY + d), NY)

    def dev(ww, yy):
        return (ww, yy)

    up_y = lax.rem(y + 2, NY)
    dn_y = lax.rem(y + NY - 2, NY)
    sib_y = y + 1 - 2 * lax.rem(y, 2)

    loads = [pltpu.make_async_copy(a, b, load_s.at[i]) for i, (a, b) in enumerate((
        (nest_hbm, nest_ref), (leg_hbm, leg_ref), (mask_hbm, mask_ref), (fold_hbm, fold_ref)))]
    for c in loads:
        c.start()

    def zero(i, c):
        pbuf[i] = jnp.zeros((KF, WIN), F32)
        return c
    lax.fori_loop(0, SLOTS, zero, 0)
    cpk_r[...] = jnp.zeros((2, 128, 128), BF16)
    rpk_r[...] = jnp.zeros((2, 96, 256), BF16)
    info_r[...] = jnp.zeros((2, 8, 128), F32)
    q_in[...] = jnp.zeros((2, 8, 768), F32)

    barrier = pltpu.get_barrier_semaphore()

    def greet(ww, yy):
        pl.semaphore_signal(barrier, inc=1, device_id=dev(ww, yy), device_id_type=MESH)

    for yy in (up_y, dn_y, sib_y):
        greet(w, yy)

    def greet_wave(o, c):
        greet(lax.rem(w + o, NW), y)
        return c
    lax.fori_loop(1, NW, greet_wave, 0)

    @pl.when(y > 0)
    def _():
        greet(w, near(-1))

    @pl.when(y < NY - 1)
    def _():
        greet(w, near(1))

    @pl.when(jnp.logical_or(jnp.logical_and(wedge, y > 0), y == NY - 1))
    def _():
        greet(NW - 1, near(-1))

    @pl.when(jnp.logical_or(jnp.logical_and(wedge, y < NY - 1), y == 0))
    def _():
        greet(0, near(1))

    sp32[0:8, :] = jnp.zeros((8, 1408), F32)
    for c in range(3):
        v = spec_ref[c].astype(F32)
        last = jnp.broadcast_to(v[:, 1280:1281], (PD, 128))
        for p0, n, r0, rows, lead in CHUNKS:
            r = r0 + lead + c * n
            sp32[r : r + n, 0:1280] = v[p0 : p0 + n, 0:1280]
            sp32[r : r + n, 1280:1408] = last[p0 : p0 + n, :]
    tail = jnp.transpose(sp32[:, 1280:1408], (1, 0))[0:8, :]
    lane = lax.broadcasted_iota(jnp.int32, (8, 128), 1)
    sub = lax.broadcasted_iota(jnp.int32, (8, 896), 0)
    extra = jnp.zeros((8, 896), F32)
    for ch, (p0, n, r0, rows, lead) in enumerate(CHUNKS):
        part = jnp.where((lane >= r0 + lead) & (lane < r0 + rows), tail, 0.0)
        part = jnp.concatenate([part, jnp.zeros((8, 768), F32)], axis=1)
        part = pltpu.roll(part, lax.rem(y * rows - r0 + 896, 896), 1)
        part = jnp.broadcast_to(part[0:1, :], (8, 896))
        extra = jnp.where(sub == ch, part, extra)
    sp32[0:8, 0:768] = extra[:, 0:768]

    def cast_own(i, c):
        r = pl.multiple_of(i * 16, 16)
        gath[y, pl.ds(r, 16), :] = sp32[pl.ds(r, 16), 0:1280].astype(BF16)
        return c
    lax.fori_loop(0, 8, cast_own, 0)

    count = 15 + 3
    count += jnp.where(y < NY - 1, 1, 0) + jnp.where(y > 0, 1, 0)
    count += jnp.where(jnp.logical_and(w == NW - 1, y < NY - 1), 2, 0)
    count += jnp.where(jnp.logical_and(w == 0, y > 0), 2, 0)
    count += jnp.where(jnp.logical_and(w == 0, y == 1), 14, 0)
    count += jnp.where(jnp.logical_and(w == NW - 1, y == NY - 2), 14, 0)
    pl.semaphore_wait(barrier, count)

    def block(origin, piece, half):
        _, _, r0, rows, _ = CHUNKS[piece]
        if half is not None:
            first, count_ = HALVES[piece][half]
            r0, rows = r0 + first, count_
        return gath.at[origin, pl.ds(r0, rows), :]

    def ring(origin, piece, step, upward):
        ref = block(origin, piece, None if step < 3 else (0 if upward else 1))
        s, r = (up_s, up_r) if upward else (dn_s, dn_r)
        return pltpu.make_async_remote_copy(
            src_ref=ref, dst_ref=ref, send_sem=s.at[piece, step], recv_sem=r.at[piece, step],
            device_id=dev(w, up_y if upward else dn_y), device_id_type=MESH)

    def to_sib(origin, piece, idx, half=None):
        ref = block(origin, piece, half)
        return pltpu.make_async_remote_copy(
            src_ref=ref, dst_ref=ref, send_sem=sib_s.at[piece, idx], recv_sem=sib_r.at[piece, idx],
            device_id=dev(w, sib_y), device_id_type=MESH)

    def origin_of(base, step, upward):
        return lax.rem(base + NY - 2 * step, NY) if upward else lax.rem(base + 2 * step, NY)

    def far(piece, upward):
        return HALVES[piece][0 if upward else 1][1] > 0

    def send_own(piece):
        ring(y, piece, 0, True).start()
        ring(y, piece, 0, False).start()
        to_sib(y, piece, 0).start()

    def ring_step(piece, step):
        for upward in (True, False):
            org = origin_of(y, step, upward)
            if step < 4:
                ring(org, piece, step - 1, upward).wait_recv()
                if step < 3 or far(piece, upward):
                    ring(org, piece, step, upward).start()
                to_sib(org, piece, 2 * step - (1 if upward else 0)).start()
            elif far(piece, upward):
                ring(org, piece, 3, upward).wait_recv()
                to_sib(org, piece, 7 if upward else 8, 0 if upward else 1).start()

    def sib_each(base, piece, go):
        go(to_sib(base, piece, 0))
        for step in range(1, 5):
            for upward in (True, False):
                org = origin_of(base, step, upward)
                if step < 4:
                    go(to_sib(org, piece, 2 * step - (1 if upward else 0)))
                elif far(piece, upward):
                    go(to_sib(org, piece, 7 if upward else 8, 0 if upward else 1))

    def sib_wait(piece):
        sib_each(sib_y, piece, lambda c: c.wait_recv())

    def sends_done(piece):
        for step in range(4):
            for upward in (True, False):
                if step < 3 or far(piece, upward):
                    ring(y, piece, step, upward).wait_send()
        sib_each(y, piece, lambda c: c.wait_send())

    anchor = anchor_ref[0].astype(F32)

    def leg_rows(ch):
        p0, n, _, _, _ = CHUNKS[ch]
        pos = lax.broadcasted_iota(jnp.int32, (1, 1280), 1)

        def one(p, c):
            limit = TRUNC - (w * PD + p0 + p)
            low = jnp.where(pos < limit, 1.0, 0.0)
            rows = leg_ref[p0 + p]
            tile = rows[:, 0:1280]
            a = pl.multiple_of(p * 16, 16)
            b = pl.multiple_of(n * 16 + p * 16, 16)
            leg2[ch % 2, pl.ds(a, 16), :] = tile * low.astype(BF16)
            leg2[ch % 2, pl.ds(b, 16), :] = tile * (1.0 - low).astype(BF16)
            last = rows[:, 1280:1281].astype(F32)
            legx[ch % 2, pl.ds(a, 16), :] = jnp.broadcast_to(last, (16, 128))
            return c
        lax.fori_loop(0, n, one, 0)

    def last_row(ch, width):
        v = gath[0, 0:16, 0:width].astype(F32)
        for i in range(1, NY):
            v = v + gath[i, 0:16, 0:width].astype(F32)
        return v[ch : ch + 1, :]

    def fourier(ch):
        p0, n, r0, rows, lead = CHUNKS[ch]
        width = 16 * rows
        g = gath[:, r0 : r0 + rows, :].reshape(width, 1280)
        x = last_row(ch, width)
        lane16 = lax.broadcasted_iota(jnp.int32, (16, 128), 1) % 16
        if ch == 0:
            res = dot_nt(leg2[0, 0:256, :], g)
            rank1 = jnp.concatenate([jnp.zeros((128, width), F32),
                                     jnp.tile(legx[0, 0:128, :], (1, width // 128)) * x], 0)
            hi, lo = split2((res + rank1) * mask_ref[...].astype(F32))
            fs[0:16] = (dot_nn(hi, fold_ref[0]) + dot_nn(lo, fold_ref[1])).reshape(16, 16, 128)
        else:
            for h in range(2):
                res = dot_nt(leg2[ch % 2, 256 * h : 256 * h + 256, :], g)
                for p in range(n):
                    v = jnp.zeros((16, 128), F32)
                    for j in range(width // 128):
                        q = res[16 * p : 16 * p + 16, 128 * j : 128 * j + 128]
                        if h == 1:
                            q = q + legx[ch % 2, 16 * p : 16 * p + 16, :] * x[:, 128 * j : 128 * j + 128]
                        q = jnp.where(lane16 == p, q, 0.0)
                        v = v + (pltpu.roll(q, (j - p) % 128, 1) if j != p else q)
                    hi = v.astype(BF16).astype(F32)
                    lo = (v - hi).astype(BF16).astype(F32)
                    fs[16 * h + p] = hi + pltpu.roll(lo, 8, 1)
        f0 = (0, 16, 48)[ch]
        for l in range(16):
            fsend[l, f0 : f0 + 2 * n, :] = fs[0 : 2 * n, l, :].astype(BF16)

    def wave_copy(ch, o):
        n = CHUNKS[ch][1]
        f0 = (0, 16, 48)[ch]
        to = lax.rem(w + o, NW)
        return pltpu.make_async_remote_copy(
            src_ref=fsend.at[to, pl.ds(f0, 2 * n), :], dst_ref=frecv.at[ch, w, pl.ds(0, 2 * n), :],
            send_sem=fa_s.at[ch, o], recv_sem=fa_r.at[ch, o],
            device_id=dev(to, y), device_id_type=MESH)

    def wave_send(ch):
        n = CHUNKS[ch][1]
        f0 = (0, 16, 48)[ch]
        lax.fori_loop(1, NW, lambda o, c: (wave_copy(ch, o).start(), c)[1], 0)
        frecv[ch, w, 0 : 2 * n, :] = fsend[w, f0 : f0 + 2 * n, :]

    def wave_recv(ch):
        lax.fori_loop(1, NW, lambda o, c: (wave_copy(ch, o).wait_recv(), c)[1], 0)

    def wave_done(ch):
        lax.fori_loop(1, NW, lambda o, c: (wave_copy(ch, o).wait_send(), c)[1], 0)

    def table(ch):
        p0, n, _, _, _ = CHUNKS[ch]
        k0 = KOFF[ch]
        shift = 4 if n == 16 else 3

        def one(t, c):
            q = t * 128 + lax.broadcasted_iota(jnp.int32, (1, 128), 1)
            ww = q >> (shift + 1)
            h = (q >> shift) & 1
            pg = ww * PD + p0 + (q & (n - 1))
            mi = jnp.where(h == 0, pg, TRUNC - 1 - pg)
            m = mi.astype(F32)
            s = jnp.where(mi == 0, 1.0, 2.0)

            def angle(x):
                return (x - NLON * jnp.floor(x * (1.0 / NLON))) * (2.0 * math.pi / NLON)

            d = lax.broadcasted_iota(jnp.int32, (LON, 128), 0).astype(F32)
            fine = angle(m * d)
            cf, sf = jnp.cos(fine) * s, jnp.sin(fine) * s
            b = lax.broadcasted_iota(jnp.int32, (16, 128), 0).astype(F32) * LON
            coarse = angle(m * (anchor + b))
            cc, sc = jnp.cos(coarse), jnp.sin(coarse)
            col = pl.multiple_of(k0 + t * 128, 128)
            for i in range(16):
                ci, si = cc[i : i + 1, :], sc[i : i + 1, :]
                vc = ci * cf - si * sf
                vs = -(si * cf + ci * sf)
                hi, lo = split2(vc)
                tcos[0, LON * i : LON * i + LON, pl.ds(col, 128)] = hi
                tcos[1, LON * i : LON * i + LON, pl.ds(col, 128)] = lo
                hi, lo = split2(vs)
                tsin[0, LON * i : LON * i + LON, pl.ds(col, 128)] = hi
                tsin[1, LON * i : LON * i + LON, pl.ds(col, 128)] = lo
            return c
        lax.fori_loop(0, 2 * n * 16 // 128, one, 0)

    def contract(ch):
        n = CHUNKS[ch][1]
        k0, k = KOFF[ch], 2 * n * 16
        f = frecv[ch, :, 0 : 2 * n, :].reshape(k, 128)

        for tab, acc in ((tcos, acc_c), (tsin, acc_s)):
            v = dot_nn(tab[0, :, k0 : k0 + k], f) + dot_nn(tab[1, :, k0 : k0 + k], f)
            if ch == 0:
                acc[...] = v
            else:
                acc[...] = acc[...] + v

    lane_h = lax.broadcasted_iota(jnp.int32, (128, 128), 1)

    def nest_copy(i):
        if i < 4:
            src, dst = (cpk_s, cpk_r) if i < 2 else (rpk_s, rpk_r)
            src, dst = src.at[i % 2], dst.at[i % 2]
        else:
            src, dst = info_s, info_r.at[i - 4]
        to = (dev(lax.rem(w + NW - 1, NW), y), dev(lax.rem(w + 1, NW), y), dev(w, near(-1)), dev(w, near(1)))[i % 4]
        return pltpu.make_async_remote_copy(
            src_ref=src, dst_ref=dst, send_sem=nest_s.at[i], recv_sem=nest_r.at[i],
            device_id=to, device_id_type=MESH)

    can_send = (w > 0, w < NW - 1, y > 0, y < NY - 1)
    can_recv = (w < NW - 1, w > 0, y < NY - 1, y > 0)

    def nest_do(which, cond, go):
        for i in which:
            @pl.when(cond[i % 4])
            def _(i=i):
                go(nest_copy(i))

    def nest_pack():
        info_s[...] = jnp.zeros((8, 128), F32)
        info_s[0:1, :] = ridx_ref[...].astype(F32)
        info_s[1:2, :] = rwt_ref[...]
        loads[0].wait()
        info_s[2:3, :] = cidx_ref[...].astype(F32)
        info_s[3:4, :] = cwt_ref[...]
        left = jnp.zeros((128, 128), F32)
        right = jnp.zeros((128, 128), F32)
        for k in range(KF):
            v = nest_ref[k].astype(F32)
            here = (lane_h >= 4 * k) & (lane_h < 4 * k + 4)
            left = jnp.where(here, pltpu.roll(v, 4 * k, 1) if k else v, left)
            right = jnp.where(here, pltpu.roll(v, 4 * k + 4, 1), right)
        cpk_s[0] = left.astype(BF16)
        cpk_s[1] = right.astype(BF16)
        row = (lax.broadcasted_iota(jnp.int32, (EXT, 256), 0) + (128 * y - 8)).astype(F32)
        j = lax.broadcasted_iota(jnp.int32, (EXT, 256), 1)
        col = (jnp.where(j < 192, j, j - 256) + 128 * w).astype(F32)
        keep, _ = shares(row, col, zone_ref)
        damp[...] = keep * DIFFUSION
        nest_do((0, 1, 4, 5), can_send, lambda c: c.start())

    def nest_cols():
        nest_do((0, 1), can_recv, lambda c: c.wait_recv())
        from_right = cpk_r[0].astype(F32)
        from_left = cpk_r[1].astype(F32)

        def one(k, c):
            a = pltpu.roll(from_right, lax.rem(128 - 4 * k, 128), 1)
            b = pltpu.roll(from_left, lax.rem(252 - 4 * k, 128), 1)
            e = jnp.where(lane_h < 4, a, jnp.where(lane_h >= 124, b, 0.0))
            ext[k, 0:8, :] = jnp.zeros((8, 256), F32)
            ext[k, 136:144, :] = jnp.zeros((8, 256), F32)
            ext[k, 8:136, 0:128] = nest_ref[k].astype(F32)
            ext[k, 8:136, 128:256] = e
            return c
        lax.fori_loop(0, KF, one, 0)
        for i, r in ((0, 8), (1, 132)):
            for k in range(KF):
                rpk[4 * k : 4 * k + 4, :] = ext[k, r : r + 4, :]
            rpk_s[i] = rpk[...].astype(BF16)
        nest_do((2, 3), can_send, lambda c: c.start())

    def nest_rows():
        nest_do((2, 3), can_recv, lambda c: c.wait_recv())
        for i, r in ((0, 136), (1, 4)):
            rpk[...] = rpk_r[i].astype(F32)
            for k in range(KF):
                ext[k, r : r + 4, :] = rpk[4 * k : 4 * k + 4, :]

    def nest_sweeps(k0, k1_):
        def one(k, c):
            x = ext[k]
            for _ in range(NSWEEP):
                t = x + pltpu.roll(x, 1, 0) + pltpu.roll(x, EXT - 1, 0)
                t = t + pltpu.roll(x, 1, 1) + pltpu.roll(x, 255, 1)
                x = t * damp[...]
            field[k] = x[8:136, 0:128]
            nest_out[k] = x[8:136, 0:128].astype(BF16)
            return c
        lax.fori_loop(k0, k1_, one, 0)

    def nest_done():
        nest_do((4, 5), can_recv, lambda c: c.wait_recv())
        nest_do(range(6), can_send, lambda c: c.wait_send())

    row_edge = jnp.logical_or(y == 0, y == NY - 1)
    first = jnp.where(y == 0, 0, 104)
    cbase = jnp.where(w == 0, 0, 96)

    def strip_prep():
        lon0 = (w * LON - 48).astype(F32)
        lat0 = (y * 16 - 1).astype(F32)
        own, right, left = info_s[...], info_r[0], info_r[1]
        lane = lax.broadcasted_iota(jnp.int32, (1, 128), 1)
        turned = jnp.transpose(jnp.concatenate([own, jnp.zeros((120, 128), F32)], 0), (1, 0))

        @pl.when(row_edge)
        def _():
            far_i = jnp.where(lane < 4, right[2:3], jnp.where(lane >= 124, left[2:3], -4096.0))
            far_w = jnp.where(lane < 4, right[3:4], left[3:4])
            cidx = jnp.concatenate([own[2:3], far_i], 1) - lon0
            cwt = jnp.concatenate([own[3:4], far_w], 1)
            hi, lo = split2(pick(fiota((128, 256), 0), cidx, cwt))
            row_mats[0] = hi
            row_mats[1] = lo
            cols = jnp.where(y == 0, turned[0:24, :], turned[104:128, :])
            ridx = cols[:, 0:1] - lat0
            rwt = cols[:, 1:2]
            row = fiota((24, 256), 0) + (128 * y + first).astype(F32)
            j = lax.broadcasted_iota(jnp.int32, (24, 256), 1)
            col = (jnp.where(j < 192, j, j - 256) + 128 * w).astype(F32)
            keep, share = shares(row, col, zone_ref)
            row_part[0] = jnp.where((row < 20.0) | (row >= 2028.0), keep * DIFFUSION, 0.0)
            row_part[1] = jnp.where((row < 16.0) | (row >= 2032.0), share, 0.0)
            for i in range(18):
                row_blend[i] = jnp.broadcast_to(pick(float(i), ridx, rwt), (24, 256))

        @pl.when(wedge)
        def _():
            vec = jnp.concatenate([own[2:4] - jnp.where(fiota((2, 128), 0) == 0.0, lon0, 0.0),
                                   jnp.zeros((6, 128), F32)], 0)
            vec = jnp.where(w == 0, vec, pltpu.roll(vec, 32, 1))
            for i in range(4):
                v = pltpu.roll(vec, LON * i, 1) if i else vec
                here = (lane >= LON * i) & (lane < LON * i + LON)
                m = jnp.where(here, pick(fiota((128, 128), 0), v[0:1], v[1:2]), 0.0)
                hi, lo = split2(m)
                col_mats[0, 128 * i : 128 * i + 128, :] = hi
                col_mats[1, 128 * i : 128 * i + 128, :] = lo
            col_blend[...] = pick(fiota((128, SLOTS), 1), turned[:, 0:1] - lat0, turned[:, 1:2])
            row = fiota((EXT, 128), 0) + (128 * y - 8).astype(F32)
            inner = lax.broadcasted_iota(jnp.int32, (EXT, 128), 1) % LON
            col = (inner + cbase + 128 * w).astype(F32)
            keep, share = shares(row, col, zone_ref)
            share = jnp.where((col < 16.0) | (col >= 2032.0), share, 0.0)
            col_part[0] = keep * DIFFUSION
            col_part[1] = jnp.where((row >= 16.0) & (row < 2032.0), share, 0.0)

    def q_copy(i):
        return pltpu.make_async_remote_copy(
            src_ref=q_out.at[i], dst_ref=q_in.at[i], send_sem=q_s.at[i], recv_sem=q_r.at[i],
            device_id=dev(w, near(1 if i else -1)), device_id_type=MESH)

    def q_each(cond, go):
        for i in range(2):
            @pl.when(jnp.logical_and(wedge, cond[i]))
            def _(i=i):
                go(q_copy(i))

    q_send = (y > 0, y < NY - 1)
    q_recv = (y < NY - 1, y > 0)

    def col_source():
        @pl.when(wedge)
        def _():
            for t in range(KF // 4):
                for i in range(4):
                    col_p[24 * t : 24 * t + 24, 128 * i : 128 * i + 128] = pbuf[:, 4 * t + i, :]
            v = dot3(col_p[...], col_mats[0], col_mats[1])
            v = jnp.concatenate([v[24 * t : 24 * t + 24, :] for t in range(KF // 4)], 1)
            hi, lo = split2(v)
            v = dot3(col_blend[...], hi, lo)
            share = col_part[1, 8:136, :]
            for t in range(KF // 4):
                col_q[8:136, 128 * t : 128 * t + 128] = v[:, 128 * t : 128 * t + 128] * share
            q_out[0] = col_q[8:16, :]
            q_out[1] = col_q[128:136, :]

        q_each(q_send, lambda c: c.start())

    def row_strip():
        @pl.when(row_edge)
        def _():
            x = dot3(pbuf[0:18].reshape(18 * KF, WIN), row_mats[0], row_mats[1])
            row_x[...] = x.reshape(18, KF, 256)
            at = pl.ds(pl.multiple_of(first, 8), 24)

            def some(n, c):
                ks = [n * 6 + i for i in range(6)]
                qs = []
                for k in ks:
                    v = jnp.zeros((24, 256), F32)
                    for i in range(18):
                        v = v + row_blend[i] * row_x[i, pl.ds(k, 1), :]
                    qs.append(v * row_part[1])
                gs = list(qs)
                for _ in range(NSWEEP - 1):
                    vs = [g + pltpu.roll(g, 1, 0) + pltpu.roll(g, 23, 0)
                          + pltpu.roll(g, 1, 1) + pltpu.roll(g, 255, 1) for g in gs]
                    gs = [v * row_part[0] + q for v, q in zip(vs, qs)]
                for k, g in zip(ks, gs):
                    field[k, at, :] = field[k, at, :] + g[:, 0:128]
                return c
            lax.fori_loop(0, KF // 6, some, 0)

    def col_strip():
        q_each(q_recv, lambda c: c.wait_recv())

        @pl.when(wedge)
        def _():
            col_q[136:144, :] = q_in[0]
            col_q[0:8, :] = q_in[1]
            inner = lax.broadcasted_iota(jnp.int32, (EXT, 128), 1) % LON
            not_first = inner != 0
            not_last = inner != LON - 1
            lane_h = lax.broadcasted_iota(jnp.int32, (128, 128), 1)
            strip = (lane_h >= cbase) & (lane_h < cbase + LON)

            def some(n, c):
                ts = [n * 2 + i for i in range(2)]
                at = [pl.ds(pl.multiple_of(t * 128, 128), 128) for t in ts]
                gs = [col_q[:, a] for a in at]
                for _ in range(NSWEEP - 1):
                    vs = [g + pltpu.roll(g, 1, 0) + pltpu.roll(g, EXT - 1, 0)
                          + jnp.where(not_first, pltpu.roll(g, 1, 1), 0.0)
                          + jnp.where(not_last, pltpu.roll(g, 127, 1), 0.0) for g in gs]
                    gs = [v * col_part[0] + col_q[:, a] for v, a in zip(vs, at)]
                for t, g in zip(ts, gs):
                    g = g[8:136, :]
                    for i in range(4):
                        part = pltpu.roll(g, lax.rem(cbase + 128 - LON * i, 128), 1)
                        field[4 * t + i] = field[4 * t + i] + jnp.where(strip, part, 0.0)
                return c
            lax.fori_loop(0, KF // 8, some, 0)

    send_own(0)
    send_own(1)
    nest_pack()
    ring_step(0, 1)
    send_own(2)
    table(0)
    table(1)
    loads[1].wait()
    leg_rows(0)
    nest_cols()
    ring_step(0, 2)
    ring_step(1, 1)
    table(2)
    nest_rows()
    leg_rows(1)
    ring_step(0, 3)
    ring_step(2, 1)
    nest_sweeps(0, 8)
    ring_step(1, 2)
    ring_step(0, 4)
    sib_wait(0)
    loads[2].wait()
    loads[3].wait()
    fourier(0)
    wave_send(0)
    ring_step(2, 2)
    nest_sweeps(8, 16)
    ring_step(1, 3)
    wave_recv(0)
    contract(0)
    ring_step(2, 3)
    nest_sweeps(16, KF)
    nest_done()
    strip_prep()
    ring_step(1, 4)
    sib_wait(1)
    leg_rows(2)
    fourier(1)
    wave_send(1)
    ring_step(2, 4)
    sib_wait(2)
    fourier(2)
    wave_send(2)
    wave_recv(1)
    contract(1)
    wave_recv(2)
    contract(2)

    prow[:, 0:128] = jnp.zeros((KF, 128), F32)
    prow[:, 512:640] = jnp.zeros((KF, 128), F32)
    for i in range(4):
        turn[0] = jnp.transpose(acc_c[128 * i : 128 * i + 128, :], (1, 0)).reshape(8, 16, 128)
        turn[1] = jnp.transpose(acc_s[128 * i : 128 * i + 128, :], (1, 0)).reshape(8, 16, 128)
        val = [turn[0, :, j, :] + turn[0, :, j + 8, :] + turn[1, :, j + 3, :] + turn[1, :, j + 11, :]
               for j in range(3)]
        prow[:, 48 + 128 * i : 176 + 128 * i] = jnp.concatenate(val, 0)
    for v in range(NW):
        psend[v] = prow[:, LON * v : LON * v + WIN]

    def win(src, to_w, to_y, slot, sem):
        return pltpu.make_async_remote_copy(
            src_ref=psend.at[src], dst_ref=pbuf.at[slot], send_sem=w_s.at[sem], recv_sem=w_r.at[slot],
            device_id=dev(to_w, to_y), device_id_type=MESH)

    def edges(go):
        @pl.when(jnp.logical_and(w == 0, y > 0))
        def _():
            go(0, 0, near(-1), 17, 16)
            go(NW - 1, NW - 1, near(-1), 17, 17)

        @pl.when(jnp.logical_and(w == NW - 1, y < NY - 1))
        def _():
            go(0, 0, near(1), 0, 18)
            go(NW - 1, NW - 1, near(1), 0, 19)

        @pl.when(jnp.logical_and(w == 0, y == 1))
        def _():
            lax.fori_loop(1, NW - 1, lambda v, c: (go(v, v, near(-1), 17, 20 + v), c)[1], 0)

        @pl.when(jnp.logical_and(w == NW - 1, y == NY - 2))
        def _():
            lax.fori_loop(1, NW - 1, lambda v, c: (go(v, v, near(1), 0, 20 + v), c)[1], 0)

    def own_win(o):
        to = lax.rem(w + o, NW)
        return win(to, to, y, 1 + w, o)

    lax.fori_loop(1, NW, lambda o, c: (own_win(o).start(), c)[1], 0)
    edges(lambda *a: win(*a).start())
    pbuf[1 + w] = psend[w]

    for ch in range(3):
        wave_done(ch)
    for piece in range(len(CHUNKS)):
        sends_done(piece)

    def got(slot):
        win(0, w, sib_y, slot, 0).wait_recv()

    lax.fori_loop(1, NW, lambda o, c: (got(1 + lax.rem(w + o, NW)), c)[1], 0)

    @pl.when(jnp.logical_or(jnp.logical_and(wedge, y > 0), y == NY - 1))
    def _():
        got(0)

    @pl.when(jnp.logical_or(jnp.logical_and(wedge, y < NY - 1), y == 0))
    def _():
        got(17)

    col_source()
    row_strip()
    col_strip()

    @pl.when(jnp.logical_or(wedge, row_edge))
    def _():
        def last(k, c):
            nest_out[k] = field[k].astype(BF16)
            return c
        lax.fori_loop(0, KF, last, 0)

    for k in range(KF):
        band_out[k] = pltpu.roll(pbuf[1:17, k, :], 80, 1)[:, 0:LON]
    q_each(q_send, lambda c: c.wait_send())
    lax.fori_loop(1, NW, lambda o, c: (own_win(o).wait_send(), c)[1], 0)
    edges(lambda *a: win(*a).wait_send())


def vmem_spec():
    return pl.BlockSpec(memory_space=pltpu.VMEM)


def spectral(spectra, legendre, lon_anchor, zone_width, nest_state, ridx, rwt, cidx, cwt):
    spec = jnp.transpose(spectra, (1, 0, 2))
    mask, fold = first_consts()
    np_ = len(CHUNKS)
    smem = pl.BlockSpec(memory_space=pltpu.SMEM)
    dma = pltpu.SemaphoreType.DMA
    return pl.pallas_call(
        k1,
        out_shape=(
            jax.ShapeDtypeStruct((KF, 16, LON), F32),
            jax.ShapeDtypeStruct((KF, 128, 128), BF16),
        ),
        in_specs=[smem, smem] + [vmem_spec()] * 5 + [pl.BlockSpec(memory_space=pl.ANY)] * 4,
        out_specs=(vmem_spec(), vmem_spec()),
        scratch_shapes=[
            pltpu.VMEM((PD, 16, 1281), BF16),
            pltpu.VMEM(mask.shape, BF16), pltpu.VMEM(fold.shape, BF16),
            pltpu.VMEM((KF, 128, 128), BF16),
            dma((4,)),
            pltpu.VMEM((NY, 128, 1280), BF16),
            pltpu.VMEM((128, 1408), F32),
            pltpu.VMEM((2, 512, 1280), BF16),
            pltpu.VMEM((2, 256, 128), F32),
            pltpu.VMEM((32, 16, 128), F32),
            pltpu.VMEM((16, 80, 128), BF16),
            pltpu.VMEM((3, 16, 32, 128), BF16),
            pltpu.VMEM((2, NLB, NKEY), BF16),
            pltpu.VMEM((2, NLB, NKEY), BF16),
            pltpu.VMEM((NLB, 128), F32),
            pltpu.VMEM((NLB, 128), F32),
            pltpu.VMEM((2, 8, 16, 128), F32),
            pltpu.VMEM((16, KF, WIN), F32),
            pltpu.VMEM((KF, 640), F32),
            pltpu.VMEM((SLOTS, KF, WIN), F32),
            pltpu.VMEM((KF, EXT, 256), F32),
            pltpu.VMEM((EXT, 256), F32),
            pltpu.VMEM((2, 128, 128), BF16),
            pltpu.VMEM((2, 128, 128), BF16),
            pltpu.VMEM((96, 256), F32),
            pltpu.VMEM((2, 96, 256), BF16),
            pltpu.VMEM((2, 96, 256), BF16),
            pltpu.VMEM((8, 128), F32),
            pltpu.VMEM((2, 8, 128), F32),
            dma((6,)), dma((6,)),
            pltpu.VMEM((KF, 128, 128), F32),
            pltpu.VMEM((2, 128, 256), BF16),
            pltpu.VMEM((2, 24, 256), F32),
            pltpu.VMEM((18, 24, 256), F32),
            pltpu.VMEM((18, KF, 256), F32),
            pltpu.VMEM((2, 512, 128), BF16),
            pltpu.VMEM((2, EXT, 128), F32),
            pltpu.VMEM((128, SLOTS), F32),
            pltpu.VMEM((144, 512), F32),
            pltpu.VMEM((EXT, 768), F32),
            pltpu.VMEM((2, 8, 768), F32),
            pltpu.VMEM((2, 8, 768), F32),
            dma((2,)), dma((2,)),
            dma((np_, 4)), dma((np_, 4)),
            dma((np_, 4)), dma((np_, 4)),
            dma((np_, 9)), dma((np_, 9)),
            dma((3, 16)), dma((3, 16)),
            dma((40,)), dma((SLOTS,)),
        ],
        compiler_params=pltpu.CompilerParams(
            collective_id=0, has_side_effects=True, vmem_limit_bytes=60 * 1024 * 1024),
    )(lon_anchor, zone_width, spec, ridx, rwt, cidx, cwt, legendre,
      jnp.asarray(mask, BF16), jnp.asarray(fold, BF16), nest_state)


def hand_over(band_in, nest_in, band_out, nest_out, band_v, nest_v, sem):
    trips = [((band_in, band_v), (band_v, band_out))]
    for i in range(4):
        at = pl.ds(6 * i, 6)
        trips.append(((nest_in.at[at], nest_v.at[at]), (nest_v.at[at], nest_out.at[at])))
    trips = [tuple(pltpu.make_async_copy(*c, sem.at[way, i]) for way, c in enumerate(trip))
             for i, trip in enumerate(trips)]
    for get, _ in trips:
        get.start()
    for get, put in trips:
        get.wait()
        put.start()
    for _, put in trips:
        put.wait()


def results(band, nest):
    hbm = pl.BlockSpec(memory_space=pl.ANY)
    return pl.pallas_call(
        hand_over,
        out_shape=(jax.ShapeDtypeStruct(band.shape, F32), jax.ShapeDtypeStruct(nest.shape, BF16)),
        in_specs=[hbm, hbm], out_specs=(hbm, hbm),
        scratch_shapes=[pltpu.VMEM(band.shape, F32), pltpu.VMEM(nest.shape, BF16),
                        pltpu.SemaphoreType.DMA((2, 5))],
        compiler_params=pltpu.CompilerParams(vmem_limit_bytes=60 * 1024 * 1024),
    )(band, nest)


def body(
    spectra, legendre, lon_anchor, row_index, row_weight, col_index, col_weight, zone_width,
    nest_state,
):
    band, nest = spectral(
        spectra, legendre, lon_anchor, zone_width, nest_state,
        row_index.reshape(1, 128), row_weight.reshape(1, 128),
        col_index.reshape(1, 128), col_weight.reshape(1, 128),
    )
    return results(band, nest)


def solution(mesh):
    placed = (
        P("wave", "ny", None), P("wave", "ny", None), P(), P("ny"), P("ny"), P("wave"), P("wave"),
        P(), P(None, "ny", "wave"),
    )
    return jax.shard_map(
        body, mesh=mesh, in_specs=placed,
        out_specs=(P(None, "ny", "wave"), P(None, "ny", "wave")), check_vma=False,
    )
```

time: 95 us -> 72.4 us (0.76)
  the two profiles are of different devices: /device:TPU:0 before, /device:TPU:1 now
where the time goes in v1:
time: 72.4 us; the launch traced here: 72.2 us
  Pallas kernels  70.9 us (98%)
  between operations  1.29 us (2%)
    pallas_call x1, Pallas kernels, spectral(): pl.pallas_call(k1, out_shape=(jax.ShapeDtypeStruct((KF, 16, LON), F32), j...  68.9 us
    pallas_call x1, Pallas kernels, results(): pl.pallas_call(hand_over, out_shape=(jax.ShapeDtypeStruct(band.shape, F32...  2.05 us

profile of v1, /device:TPU:1, one launch (start us, length us, event | category | flops | bytes accessed | tf_op | source)
XLA Modules:
  0.0 72.2 jit_solution(5197239329725204269)
XLA Ops:
  1.3 68.9 %shard_map.122 = (f32[24,16,32]{2,1,0:T(8,128)}, bf16[24,128,128]{2,1,0:T(8,128)(2,1)}) custom-call(s32[1]{0:T(128)S(6)} %copy.13.anchor_ref, s32[4]{0:T(128)} %zone_ref.1, bf16[3,40,1281]{2,1,0:T(8,128)(2,1)} %bitcast.5, s32[1,128]{1,0:T(1,128)} %bitcast.6, f32[1,128]{1,0:T(1,128)} %bitcast.7, s32[1,128]{1,0:T(1,128)} %bitcast.8, f32[1,128]{1,0:T(1,128)} %bitcast.9, ...), custom_call_target="tpu_custom_call" | custom-call | tf_op jit(solution)/shard_map/pallas_call | solution.py:754
  70.2 2.0 %shard_map.123 = (f32[24,16,32]{2,1,0:T(8,128)}, bf16[24,128,128]{2,1,0:T(8,128)(2,1)}) custom-call(f32[24,16,32]{2,1,0:T(8,128)} %get-tuple-element.4.band_in, bf16[24,128,128]{2,1,0:T(8,128)(2,1)} %get-tuple-element.5.nest_in), custom_call_target="tpu_custom_call" | custom-call | tf_op jit(solution)/shard_map/pallas_call | solution.py:835

commit v2 on v1

--- a/solution.py
+++ b/solution.py
@@ -99,9 +99,9 @@
     leg_hbm, mask_hbm, fold_hbm, nest_hbm,
     band_out, nest_out,
     leg_ref, mask_ref, fold_ref, nest_ref, load_s,
-    gath, sp32, leg2, legx, fs, fsend, frecv, tcos, tsin, acc_c, acc_s, turn, psend, prow, pbuf,
+    gath, sp32, leg2, legx, fs, fsend, frecv, tcos, tsin, acc_c, acc_s, turn, psend, pack_s, pack_r, prow, pbuf,
     ext, damp, cpk_s, cpk_r, rpk, rpk_s, rpk_r, info_s, info_r, nest_s, nest_r,
-    field, row_mats, row_part, row_blend, row_x, col_mats, col_part, col_blend, col_p, col_q,
+    field, row_mats, row_part, row_blend, row_x, col_mats, col_part, col_blend, lats, col_q,
     q_out, q_in, q_s, q_r,
     up_s, up_r, dn_s, dn_r, sib_s, sib_r, fa_s, fa_r, w_s, w_r,
 ):
@@ -503,8 +503,7 @@
             keep, share = shares(row, col, zone_ref)
             row_part[0] = jnp.where((row < 20.0) | (row >= 2028.0), keep * DIFFUSION, 0.0)
             row_part[1] = jnp.where((row < 16.0) | (row >= 2032.0), share, 0.0)
-            for i in range(18):
-                row_blend[i] = jnp.broadcast_to(pick(float(i), ridx, rwt), (24, 256))
+            row_blend[...] = pick(fiota((24, SLOTS), 1), ridx, rwt)
 
         @pl.when(wedge)
         def _():
@@ -541,17 +540,21 @@
     q_send = (y > 0, y < NY - 1)
     q_recv = (y < NY - 1, y > 0)
 
+    def gather_rows():
+        for k in range(KF):
+            lats[:, 128 * k : 128 * k + 128] = pbuf[:, k, :]
+
     def col_source():
         @pl.when(wedge)
         def _():
-            for t in range(KF // 4):
-                for i in range(4):
-                    col_p[24 * t : 24 * t + 24, 128 * i : 128 * i + 128] = pbuf[:, 4 * t + i, :]
-            v = dot3(col_p[...], col_mats[0], col_mats[1])
+            v = jnp.concatenate([lats[:, 512 * t : 512 * t + 512] for t in range(KF // 4)], 0)
+            v = dot3(v, col_mats[0], col_mats[1])
             v = jnp.concatenate([v[24 * t : 24 * t + 24, :] for t in range(KF // 4)], 1)
             hi, lo = split2(v)
             v = dot3(col_blend[...], hi, lo)
             share = col_part[1, 8:136, :]
+            col_q[0:8, :] = jnp.zeros((8, 768), F32)
+            col_q[136:144, :] = jnp.zeros((8, 768), F32)
             for t in range(KF // 4):
                 col_q[8:136, 128 * t : 128 * t + 128] = v[:, 128 * t : 128 * t + 128] * share
             q_out[0] = col_q[8:16, :]
@@ -562,18 +565,15 @@
     def row_strip():
         @pl.when(row_edge)
         def _():
-            x = dot3(pbuf[0:18].reshape(18 * KF, WIN), row_mats[0], row_mats[1])
-            row_x[...] = x.reshape(18, KF, 256)
+            hi, lo = split2(lats[...])
+            v = dot3(row_blend[...], hi, lo)
+            v = jnp.concatenate([v[:, 128 * k : 128 * k + 128] for k in range(KF)], 0)
+            row_x[...] = dot3(v, row_mats[0], row_mats[1])
             at = pl.ds(pl.multiple_of(first, 8), 24)
 
             def some(n, c):
                 ks = [n * 6 + i for i in range(6)]
-                qs = []
-                for k in ks:
-                    v = jnp.zeros((24, 256), F32)
-                    for i in range(18):
-                        v = v + row_blend[i] * row_x[i, pl.ds(k, 1), :]
-                    qs.append(v * row_part[1])
+                qs = [row_x[pl.ds(pl.multiple_of(k * 24, 8), 24), :] * row_part[1] for k in ks]
                 gs = list(qs)
                 for _ in range(NSWEEP - 1):
                     vs = [g + pltpu.roll(g, 1, 0) + pltpu.roll(g, 23, 0)
@@ -584,35 +584,67 @@
                 return c
             lax.fori_loop(0, KF // 6, some, 0)
 
+        @pl.when(jnp.logical_and(row_edge, jnp.logical_not(wedge)))
+        def _():
+            at = pl.ds(pl.multiple_of(jnp.where(y == 0, 0, 96), 32), 32)
+
+            def last(k, c):
+                nest_out[k, at, :] = field[k, at, :].astype(BF16)
+                return c
+            lax.fori_loop(0, KF, last, 0)
+
+    def side_masks(rows):
+        inner = lax.broadcasted_iota(jnp.int32, (rows, 128), 1) % LON
+        return inner != 0, inner != LON - 1
+
+    def side_sweeps(qs, keep, rows):
+        not_first, not_last = side_masks(rows)
+        gs = list(qs)
+        for _ in range(NSWEEP - 1):
+            vs = [g + pltpu.roll(g, 1, 0) + pltpu.roll(g, rows - 1, 0)
+                  + jnp.where(not_first, pltpu.roll(g, 1, 1), 0.0)
+                  + jnp.where(not_last, pltpu.roll(g, 127, 1), 0.0) for g in gs]
+            gs = [v * keep + q for v, q in zip(vs, qs)]
+        return gs
+
     def col_strip():
+        @pl.when(wedge)
+        def _():
+            def some(n, c):
+                at = [pl.ds(pl.multiple_of((n * 2 + i) * 128, 128), 128) for i in range(2)]
+                gs = side_sweeps([col_q[:, a] for a in at], col_part[0], EXT)
+                for a, g in zip(at, gs):
+                    col_q[:, a] = g
+                return c
+            lax.fori_loop(0, KF // 8, some, 0)
+
         q_each(q_recv, lambda c: c.wait_recv())
 
         @pl.when(wedge)
         def _():
-            col_q[136:144, :] = q_in[0]
-            col_q[0:8, :] = q_in[1]
-            inner = lax.broadcasted_iota(jnp.int32, (EXT, 128), 1) % LON
-            not_first = inner != 0
-            not_last = inner != LON - 1
+            sub = lax.broadcasted_iota(jnp.int32, (8, 768), 0)
+            blank = jnp.zeros((8, 768), F32)
+            above = jnp.concatenate([jnp.where(sub >= 4, q_in[1], 0.0), blank], 0)
+            below = jnp.concatenate([blank, jnp.where(sub < 4, q_in[0], 0.0)], 0)
+            tiles = range(KF // 4)
+            ga = side_sweeps([above[:, 128 * t : 128 * t + 128] for t in tiles], col_part[0, 0:16, :], 16)
+            gb = side_sweeps([below[:, 128 * t : 128 * t + 128] for t in tiles], col_part[0, 128:144, :], 16)
+            for t in tiles:
+                a = slice(128 * t, 128 * t + 128)
+                col_q[8:16, a] = col_q[8:16, a] + ga[t][8:16]
+                col_q[128:136, a] = col_q[128:136, a] + gb[t][0:8]
             lane_h = lax.broadcasted_iota(jnp.int32, (128, 128), 1)
             strip = (lane_h >= cbase) & (lane_h < cbase + LON)
 
-            def some(n, c):
-                ts = [n * 2 + i for i in range(2)]
-                at = [pl.ds(pl.multiple_of(t * 128, 128), 128) for t in ts]
-                gs = [col_q[:, a] for a in at]
-                for _ in range(NSWEEP - 1):
-                    vs = [g + pltpu.roll(g, 1, 0) + pltpu.roll(g, EXT - 1, 0)
-                          + jnp.where(not_first, pltpu.roll(g, 1, 1), 0.0)
-                          + jnp.where(not_last, pltpu.roll(g, 127, 1), 0.0) for g in gs]
-                    gs = [v * col_part[0] + col_q[:, a] for v, a in zip(vs, at)]
-                for t, g in zip(ts, gs):
-                    g = g[8:136, :]
+            def add(n, c):
+                for t in (n * 2, n * 2 + 1):
+                    g = col_q[8:136, pl.ds(pl.multiple_of(t * 128, 128), 128)]
                     for i in range(4):
                         part = pltpu.roll(g, lax.rem(cbase + 128 - LON * i, 128), 1)
-                        field[4 * t + i] = field[4 * t + i] + jnp.where(strip, part, 0.0)
+                        k = 4 * t + i
+                        nest_out[k] = (field[k] + jnp.where(strip, part, 0.0)).astype(BF16)
                 return c
-            lax.fori_loop(0, KF // 8, some, 0)
+            lax.fori_loop(0, KF // 8, add, 0)
 
     send_own(0)
     send_own(1)
@@ -649,11 +681,11 @@
     nest_done()
     strip_prep()
     ring_step(1, 4)
+    leg_rows(2)
+    ring_step(2, 4)
     sib_wait(1)
-    leg_rows(2)
     fourier(1)
     wave_send(1)
-    ring_step(2, 4)
     sib_wait(2)
     fourier(2)
     wave_send(2)
@@ -670,8 +702,15 @@
         val = [turn[0, :, j, :] + turn[0, :, j + 8, :] + turn[1, :, j + 3, :] + turn[1, :, j + 11, :]
                for j in range(3)]
         prow[:, 48 + 128 * i : 176 + 128 * i] = jnp.concatenate(val, 0)
+    lane = lax.broadcasted_iota(jnp.int32, (8, 128), 1)
     for v in range(NW):
-        psend[v] = prow[:, LON * v : LON * v + WIN]
+        window = prow[:, LON * v : LON * v + WIN]
+        psend[v] = window
+        packed = jnp.zeros((8, 128), F32)
+        for j in range(3):
+            part = pltpu.roll(window[8 * j : 8 * j + 8], (LON * j + 80) % 128, 1)
+            packed = jnp.where((lane >= LON * j) & (lane < LON * j + LON), part, packed)
+        pack_s[v] = packed
 
     def win(src, to_w, to_y, slot, sem):
         return pltpu.make_async_remote_copy(
@@ -701,9 +740,31 @@
         to = lax.rem(w + o, NW)
         return win(to, to, y, 1 + w, o)
 
-    lax.fori_loop(1, NW, lambda o, c: (own_win(o).start(), c)[1], 0)
+    def own_pack(o):
+        to = lax.rem(w + o, NW)
+        return pltpu.make_async_remote_copy(
+            src_ref=pack_s.at[to], dst_ref=pack_r.at[w], send_sem=w_s.at[o], recv_sem=w_r.at[1 + w],
+            device_id=dev(to, y), device_id_type=MESH)
+
+    def own_each(go):
+        def one(o, c):
+            to = lax.rem(w + o, NW)
+            whole = jnp.logical_or(row_edge, jnp.logical_or(to == 0, to == NW - 1))
+
+            @pl.when(whole)
+            def _():
+                go(own_win(o))
+
+            @pl.when(jnp.logical_not(whole))
+            def _():
+                go(own_pack(o))
+            return c
+        lax.fori_loop(1, NW, one, 0)
+
+    own_each(lambda c: c.start())
     edges(lambda *a: win(*a).start())
     pbuf[1 + w] = psend[w]
+    pack_r[w] = pack_s[w]
 
     for ch in range(3):
         wave_done(ch)
@@ -713,7 +774,21 @@
     def got(slot):
         win(0, w, sib_y, slot, 0).wait_recv()
 
-    lax.fori_loop(1, NW, lambda o, c: (got(1 + lax.rem(w + o, NW)), c)[1], 0)
+    here_whole = jnp.logical_or(row_edge, wedge)
+
+    @pl.when(here_whole)
+    def _():
+        lax.fori_loop(1, NW, lambda o, c: (got(1 + lax.rem(w + o, NW)), c)[1], 0)
+
+    @pl.when(jnp.logical_not(here_whole))
+    def _():
+        def one(o, c):
+            src = lax.rem(w + o, NW)
+            pltpu.make_async_remote_copy(
+                src_ref=pack_s.at[0], dst_ref=pack_r.at[src], send_sem=w_s.at[0],
+                recv_sem=w_r.at[1 + src], device_id=dev(w, sib_y), device_id_type=MESH).wait_recv()
+            return c
+        lax.fori_loop(1, NW, one, 0)
 
     @pl.when(jnp.logical_or(jnp.logical_and(wedge, y > 0), y == NY - 1))
     def _():
@@ -722,22 +797,29 @@
     @pl.when(jnp.logical_or(jnp.logical_and(wedge, y < NY - 1), y == 0))
     def _():
         got(17)
+
+    @pl.when(here_whole)
+    def _():
+        gather_rows()
 
     col_source()
     row_strip()
     col_strip()
 
-    @pl.when(jnp.logical_or(wedge, row_edge))
-    def _():
-        def last(k, c):
-            nest_out[k] = field[k].astype(BF16)
-            return c
-        lax.fori_loop(0, KF, last, 0)
-
-    for k in range(KF):
-        band_out[k] = pltpu.roll(pbuf[1:17, k, :], 80, 1)[:, 0:LON]
+    @pl.when(here_whole)
+    def _():
+        for k in range(KF):
+            band_out[k] = pltpu.roll(pbuf[1:17, k, :], 80, 1)[:, 0:LON]
+
+    @pl.when(jnp.logical_not(here_whole))
+    def _():
+        for i in range(8):
+            v = pack_r[:, i, :]
+            for j in range(3):
+                band_out[8 * j + i] = (pltpu.roll(v, 128 - LON * j, 1) if j else v)[:, 0:LON]
+
     q_each(q_send, lambda c: c.wait_send())
-    lax.fori_loop(1, NW, lambda o, c: (own_win(o).wait_send(), c)[1], 0)
+    own_each(lambda c: c.wait_send())
     edges(lambda *a: win(*a).wait_send())
 
 
@@ -777,6 +859,8 @@
             pltpu.VMEM((NLB, 128), F32),
             pltpu.VMEM((2, 8, 16, 128), F32),
             pltpu.VMEM((16, KF, WIN), F32),
+            pltpu.VMEM((16, 8, 128), F32),
+            pltpu.VMEM((16, 8, 128), F32),
             pltpu.VMEM((KF, 640), F32),
             pltpu.VMEM((SLOTS, KF, WIN), F32),
             pltpu.VMEM((KF, EXT, 256), F32),
@@ -792,12 +876,12 @@
             pltpu.VMEM((KF, 128, 128), F32),
             pltpu.VMEM((2, 128, 256), BF16),
             pltpu.VMEM((2, 24, 256), F32),
-            pltpu.VMEM((18, 24, 256), F32),
-            pltpu.VMEM((18, KF, 256), F32),
+            pltpu.VMEM((24, SLOTS), F32),
+            pltpu.VMEM((24 * KF, 256), F32),
             pltpu.VMEM((2, 512, 128), BF16),
             pltpu.VMEM((2, EXT, 128), F32),
             pltpu.VMEM((128, SLOTS), F32),
-            pltpu.VMEM((144, 512), F32),
+            pltpu.VMEM((SLOTS, 128 * KF), F32),
             pltpu.VMEM((EXT, 768), F32),
             pltpu.VMEM((2, 8, 768), F32),
             pltpu.VMEM((2, 8, 768), F32),

time: 72.4 us -> 69.9 us (0.965)
  Pallas kernels: 70.9 us -> 68.4 us
    pallas_call x1, Pallas kernels: 68.9 us -> 66.4 us  [spectral(): pl.pallas_call(k1, out_shape=(jax.ShapeDtypeStruct((KF, 16, LON), F32), j...]
where the time goes in v2:
time: 69.9 us; the launch traced here: 69.7 us
  Pallas kernels  68.4 us (98%)
  between operations  1.29 us (2%)
    pallas_call x1, Pallas kernels, spectral(): pl.pallas_call(k1, out_shape=(jax.ShapeDtypeStruct((KF, 16, LON), F32), j...  66.4 us
    pallas_call x1, Pallas kernels, results(): pl.pallas_call(hand_over, out_shape=(jax.ShapeDtypeStruct(band.shape, F32...  2.05 us

profile of v2, /device:TPU:1, one launch (start us, length us, event | category | flops | bytes accessed | tf_op | source)
XLA Modules:
  0.0 69.7 jit_solution(12884135067657819549)
XLA Ops:
  1.3 66.4 %shard_map.122 = (f32[24,16,32]{2,1,0:T(8,128)}, bf16[24,128,128]{2,1,0:T(8,128)(2,1)}) custom-call(s32[1]{0:T(128)S(6)} %copy.13.anchor_ref, s32[4]{0:T(128)} %zone_ref.1, bf16[3,40,1281]{2,1,0:T(8,128)(2,1)} %bitcast.5, s32[1,128]{1,0:T(1,128)} %bitcast.6, f32[1,128]{1,0:T(1,128)} %bitcast.7, s32[1,128]{1,0:T(1,128)} %bitcast.8, f32[1,128]{1,0:T(1,128)} %bitcast.9, ...), custom_call_target="tpu_custom_call" | custom-call | tf_op jit(solution)/shard_map/pallas_call | solution.py:836
  67.7 2.0 %shard_map.123 = (f32[24,16,32]{2,1,0:T(8,128)}, bf16[24,128,128]{2,1,0:T(8,128)(2,1)}) custom-call(f32[24,16,32]{2,1,0:T(8,128)} %get-tuple-element.4.band_in, bf16[24,128,128]{2,1,0:T(8,128)(2,1)} %get-tuple-element.5.nest_in), custom_call_target="tpu_custom_call" | custom-call | tf_op jit(solution)/shard_map/pallas_call | solution.py:919

commit v3 on v2

--- a/solution.py
+++ b/solution.py
@@ -651,13 +651,13 @@
     nest_pack()
     ring_step(0, 1)
     send_own(2)
+    nest_cols()
     table(0)
+    ring_step(0, 2)
+    ring_step(1, 1)
     table(1)
     loads[1].wait()
     leg_rows(0)
-    nest_cols()
-    ring_step(0, 2)
-    ring_step(1, 1)
     table(2)
     nest_rows()
     leg_rows(1)
@@ -685,8 +685,8 @@
     ring_step(2, 4)
     sib_wait(1)
     fourier(1)
+    sib_wait(2)
     wave_send(1)
-    sib_wait(2)
     fourier(2)
     wave_send(2)
     wave_recv(1)
@@ -710,6 +710,10 @@
         for j in range(3):
             part = pltpu.roll(window[8 * j : 8 * j + 8], (LON * j + 80) % 128, 1)
             packed = jnp.where((lane >= LON * j) & (lane < LON * j + LON), part, packed)
+            if v in (0, NW - 1):
+                beside = 80 if v == 0 else 47
+                part = pltpu.roll(window[8 * j : 8 * j + 8], (96 + j - beside) % 128, 1)
+                packed = jnp.where(lane == 96 + j, part, packed)
         pack_s[v] = packed
 
     def win(src, to_w, to_y, slot, sem):
@@ -747,19 +751,13 @@
             device_id=dev(to, y), device_id_type=MESH)
 
     def own_each(go):
-        def one(o, c):
-            to = lax.rem(w + o, NW)
-            whole = jnp.logical_or(row_edge, jnp.logical_or(to == 0, to == NW - 1))
-
-            @pl.when(whole)
-            def _():
-                go(own_win(o))
-
-            @pl.when(jnp.logical_not(whole))
-            def _():
-                go(own_pack(o))
-            return c
-        lax.fori_loop(1, NW, one, 0)
+        @pl.when(row_edge)
+        def _():
+            lax.fori_loop(1, NW, lambda o, c: (go(own_win(o)), c)[1], 0)
+
+        @pl.when(jnp.logical_not(row_edge))
+        def _():
+            lax.fori_loop(1, NW, lambda o, c: (go(own_pack(o)), c)[1], 0)
 
     own_each(lambda c: c.start())
     edges(lambda *a: win(*a).start())
@@ -774,7 +772,7 @@
     def got(slot):
         win(0, w, sib_y, slot, 0).wait_recv()
 
-    here_whole = jnp.logical_or(row_edge, wedge)
+    here_whole = row_edge
 
     @pl.when(here_whole)
     def _():
@@ -798,7 +796,17 @@
     def _():
         got(17)
 
-    @pl.when(here_whole)
+    @pl.when(jnp.logical_and(wedge, jnp.logical_not(row_edge)))
+    def _():
+        beside = jnp.where(w == 0, 80, 47)
+        for s in range(16):
+            for j in range(3):
+                a = pltpu.roll(pack_r[s], (48 - LON * j) % 128, 1)
+                b = pltpu.roll(pack_r[s], lax.rem(beside + 128 - 96 - j + 128, 128), 1)
+                a = jnp.where((lane >= 48) & (lane < 80), a, jnp.where(lane == beside, b, 0.0))
+                pbuf[1 + s, 8 * j : 8 * j + 8, :] = a
+
+    @pl.when(jnp.logical_or(wedge, row_edge))
     def _():
         gather_rows()
 

time: 69.9 us -> 69.1 us (0.989)
  Pallas kernels: 68.4 us -> 67.7 us
    pallas_call x1, Pallas kernels: 66.4 us -> 65.7 us  [spectral(): pl.pallas_call(k1, out_shape=(jax.ShapeDtypeStruct((KF, 16, LON), F32), j...]
where the time goes in v3:
time: 69.1 us; the launch traced here: 69 us
  Pallas kernels  67.7 us (98%)
  between operations  1.29 us (2%)
    pallas_call x1, Pallas kernels, spectral(): pl.pallas_call(k1, out_shape=(jax.ShapeDtypeStruct((KF, 16, LON), F32), j...  65.7 us
    pallas_call x1, Pallas kernels, results(): pl.pallas_call(hand_over, out_shape=(jax.ShapeDtypeStruct(band.shape, F32...  2.05 us

profile of v3, /device:TPU:1, one launch (start us, length us, event | category | flops | bytes accessed | tf_op | source)
XLA Modules:
  0.0 69.0 jit_solution(15000505650699745563)
XLA Ops:
  1.3 65.7 %shard_map.122 = (f32[24,16,32]{2,1,0:T(8,128)}, bf16[24,128,128]{2,1,0:T(8,128)(2,1)}) custom-call(s32[1]{0:T(128)S(6)} %copy.13.anchor_ref, s32[4]{0:T(128)} %zone_ref.1, bf16[3,40,1281]{2,1,0:T(8,128)(2,1)} %bitcast.5, s32[1,128]{1,0:T(1,128)} %bitcast.6, f32[1,128]{1,0:T(1,128)} %bitcast.7, s32[1,128]{1,0:T(1,128)} %bitcast.8, f32[1,128]{1,0:T(1,128)} %bitcast.9, ...), custom_call_target="tpu_custom_call" | custom-call | tf_op jit(solution)/shard_map/pallas_call | solution.py:844
  67.0 2.0 %shard_map.123 = (f32[24,16,32]{2,1,0:T(8,128)}, bf16[24,128,128]{2,1,0:T(8,128)(2,1)}) custom-call(f32[24,16,32]{2,1,0:T(8,128)} %get-tuple-element.4.band_in, bf16[24,128,128]{2,1,0:T(8,128)(2,1)} %get-tuple-element.5.nest_in), custom_call_target="tpu_custom_call" | custom-call | tf_op jit(solution)/shard_map/pallas_call | solution.py:927

commit v4 on v3

--- a/solution.py
+++ b/solution.py
@@ -759,8 +759,8 @@
         def _():
             lax.fori_loop(1, NW, lambda o, c: (go(own_pack(o)), c)[1], 0)
 
+    edges(lambda *a: win(*a).start())
     own_each(lambda c: c.start())
-    edges(lambda *a: win(*a).start())
     pbuf[1 + w] = psend[w]
     pack_r[w] = pack_s[w]
 

time: 69.1 us -> 69.1 us (level)
  no operation moved by 1% of the time
where the time goes in v4:
time: 69.1 us; the launch traced here: 69 us
  Pallas kernels  67.7 us (98%)
  between operations  1.29 us (2%)
    pallas_call x1, Pallas kernels, spectral(): pl.pallas_call(k1, out_shape=(jax.ShapeDtypeStruct((KF, 16, LON), F32), j...  65.7 us
    pallas_call x1, Pallas kernels, results(): pl.pallas_call(hand_over, out_shape=(jax.ShapeDtypeStruct(band.shape, F32...  2.05 us

profile of v4, /device:TPU:1, one launch (start us, length us, event | category | flops | bytes accessed | tf_op | source)
XLA Modules:
  0.0 69.0 jit_solution(17961926364419838522)
XLA Ops:
  1.3 65.7 %shard_map.122 = (f32[24,16,32]{2,1,0:T(8,128)}, bf16[24,128,128]{2,1,0:T(8,128)(2,1)}) custom-call(s32[1]{0:T(128)S(6)} %copy.13.anchor_ref, s32[4]{0:T(128)} %zone_ref.1, bf16[3,40,1281]{2,1,0:T(8,128)(2,1)} %bitcast.5, s32[1,128]{1,0:T(1,128)} %bitcast.6, f32[1,128]{1,0:T(1,128)} %bitcast.7, s32[1,128]{1,0:T(1,128)} %bitcast.8, f32[1,128]{1,0:T(1,128)} %bitcast.9, ...), custom_call_target="tpu_custom_call" | custom-call | tf_op jit(solution)/shard_map/pallas_call | solution.py:844
  67.0 2.0 %shard_map.123 = (f32[24,16,32]{2,1,0:T(8,128)}, bf16[24,128,128]{2,1,0:T(8,128)(2,1)}) custom-call(f32[24,16,32]{2,1,0:T(8,128)} %get-tuple-element.4.band_in, bf16[24,128,128]{2,1,0:T(8,128)(2,1)} %get-tuple-element.5.nest_in), custom_call_target="tpu_custom_call" | custom-call | tf_op jit(solution)/shard_map/pallas_call | solution.py:927
